TPU v7x, 512 devices: a whole 4x8x8 slice. The times are simulated.
512 devices in a mesh: ctx: 32 (over y_hi, z, core), tp: 16 (over y_lo, x).
Axes of the slice: x: 4, y: 8 (y_hi: 2, y_lo: 4; y = y_hi * 4 + y_lo), z: 8, core: 2. Of those that a mesh axis runs over, the one named last changes fastest.
Arguments:
- queries: bfloat16 [4096, 8192], P('ctx', 'tp'), may hold values from -6 to 6
- keys_in: bfloat16 [4096, 8192], P('ctx', 'tp'), may hold values from -6 to 6
- values_in: bfloat16 [4096, 8192], P('ctx', 'tp'), may hold values from -6 to 6
- decay_rates: float32 [8192, 16], P('tp'), may hold values from 7.324219e-05 to 0.03
- residues: float32 [8192, 16], P('tp'), may hold values from -1.5 to 1.5
- skip_gain: float32 [8192], P('tp'), may hold values from -4 to 4
- cotangent: bfloat16 [4096, 8192], P('ctx', 'tp'), may hold values from -6 to 6
Outputs:
- operator_out: bfloat16 [4096, 8192], P('ctx', 'tp')
- grad_queries: bfloat16 [4096, 8192], P('ctx', 'tp')
- grad_keys: bfloat16 [4096, 8192], P('ctx', 'tp')
- grad_values: bfloat16 [4096, 8192], P('ctx', 'tp')
- grad_residues: float32 [8192, 16], P('tp')
All inputs are finite; a program needn't handle non-finite values.
Results may differ from a plain program's by a relative error of at most 0.0054.
Values may be sent and summed in bfloat16 or wider, within the bound.
A program may use at most 64 MiB of HBM per device.

v0:
```python
from functools import partial
import math

import jax
import jax.numpy as jnp
from jax import lax
from jax.sharding import PartitionSpec as P

D = 8192
ORDER = 16


PRECISE = lax.Precision.HIGHEST


def chain_link(earlier_pair, later_pair):
    return (earlier_pair[0] * later_pair[0], later_pair[0] * earlier_pair[1] + later_pair[1])


def prepare(decay, weight, block_len):
    positions = jnp.arange(block_len + 1, dtype=jnp.float32)
    powers = jnp.exp(-decay[None] * positions[:, None, None])
    unit_scale = jnp.sqrt(1.0 - jnp.exp(-2.0 * decay))
    mode_coef = weight * unit_scale
    short_filter = jnp.einsum("kcn,cn->kc", powers[:block_len], mode_coef, precision=PRECISE)
    lag_table = jnp.arange(block_len)[:, None] - jnp.arange(block_len)[None, :]
    toeplitz = jnp.where((lag_table >= 0)[:, :, None], short_filter[jnp.maximum(lag_table, 0)], 0.0)
    return (positions, powers, unit_scale, mode_coef, toeplitz, lag_table)


def forward_states(in_blocks, powers, decay, carry_in, block_len):
    block_count = in_blocks.shape[0]
    end_states = jnp.einsum("bsc,scn->bcn", in_blocks, powers[:block_len][::-1], precision=PRECISE)
    decays = jnp.broadcast_to(powers[block_len], end_states.shape)
    _, totals = lax.associative_scan(chain_link, (decays, end_states), axis=0)
    distance = block_len * jnp.arange(1, block_count + 1, dtype=jnp.float32)
    states = totals + jnp.exp(-decay[None] * distance[:, None, None]) * carry_in[None]
    before = jnp.concatenate([carry_in[None], states[:-1]], 0)
    return (before, totals[-1])


def backward_states(back_blocks, powers, decay, carry_back, block_len):
    block_count = back_blocks.shape[0]
    start_states = jnp.einsum("btc,tcn->bcn", back_blocks, powers[:block_len], precision=PRECISE)
    decays = jnp.broadcast_to(powers[block_len], start_states.shape)
    _, totals = lax.associative_scan(chain_link, (decays[::-1], start_states[::-1]), axis=0)
    totals = totals[::-1]
    distance = block_len * jnp.arange(block_count, 0, -1, dtype=jnp.float32)
    states = totals + jnp.exp(-decay[None] * distance[:, None, None]) * carry_back[None]
    after = jnp.concatenate([states[1:], carry_back[None]], 0)
    return (after, totals[0])


def forward_work(lines, tables, block_len):
    decay, weight, carry_in = tables
    positions, powers, unit_scale, mode_coef, toeplitz, lag_table = prepare(
        decay, weight, block_len
    )
    in_blocks = lines[0].reshape(-1, block_len, lines[0].shape[1])
    before, _ = forward_states(in_blocks, powers, decay, carry_in, block_len)
    within_block = jnp.einsum("bsc,tsc->btc", in_blocks, toeplitz, precision=PRECISE)
    from_carry = jnp.einsum("bcn,tcn->btc", before, powers[1:] * mode_coef[None], precision=PRECISE)
    return (within_block + from_carry).reshape(lines[0].shape)


def backward_work(lines, tables, block_len):
    decay, weight, carry_in, carry_back = tables
    positions, powers, unit_scale, mode_coef, toeplitz, lag_table = prepare(
        decay, weight, block_len
    )
    in_blocks = lines[0].reshape(-1, block_len, lines[0].shape[1])
    back_blocks = lines[1].reshape(-1, block_len, lines[1].shape[1])
    before, _ = forward_states(in_blocks, powers, decay, carry_in, block_len)
    after, _ = backward_states(back_blocks, powers, decay, carry_back, block_len)
    within_block = jnp.einsum("btc,tsc->bsc", back_blocks, toeplitz, precision=PRECISE)
    from_carry = jnp.einsum(
        "bcn,scn->bsc", after, powers[1:][::-1] * mode_coef[None], precision=PRECISE
    )
    adjoint = (within_block + from_carry).reshape(lines[1].shape)
    carried = jnp.einsum("btc,tcn,bcn->cn", back_blocks, powers[1:], before, precision=PRECISE)
    pairs = jnp.einsum("btc,bsc->tsc", back_blocks, in_blocks, precision=PRECISE)
    pairs = jnp.where((lag_table >= 0)[:, :, None], pairs, 0.0)
    rising = jnp.exp(decay[None] * positions[:block_len, None, None])
    inside = jnp.einsum("tsc,tcn,scn->cn", pairs, powers[:block_len], rising, precision=PRECISE)
    return (adjoint, unit_scale * (carried + inside))


def to_groups(line_array, group_width):
    seq_rows, channels = line_array.shape
    return jnp.moveaxis(line_array.reshape(seq_rows, channels // group_width, group_width), 1, 0)


def from_groups(stacked):
    group_count, seq_rows, group_width = stacked.shape
    return jnp.moveaxis(stacked, 0, 1).reshape(seq_rows, group_count * group_width)


def param_groups(param_table, group_width):
    return param_table.reshape(
        param_table.shape[0] // group_width, group_width, param_table.shape[1]
    )


def grouped(work_fn, lines, tables, group_width):
    stacked_lines = tuple((to_groups(item, group_width) for item in lines))
    stacked_tables = tuple((param_groups(item, group_width) for item in tables))
    return lax.map(lambda packed: work_fn(packed[0], packed[1]), (stacked_lines, stacked_tables))


def flat_table(stacked):
    return stacked.reshape(stacked.shape[0] * stacked.shape[1], stacked.shape[2])


def shards(queries, keys_in, values_in, decay_rates, residues, skip_gain, cotangent):
    seq_rows, channels = queries.shape
    mode_count = decay_rates.shape[1]
    queries_f = queries.astype(jnp.float32)
    keys_f = keys_in.astype(jnp.float32)
    values_f = values_in.astype(jnp.float32)
    cot_f = cotangent.astype(jnp.float32)
    gated = lax.optimization_barrier((keys_f * values_f).astype(jnp.bfloat16))
    pulled = lax.optimization_barrier((cot_f * queries_f).astype(jnp.bfloat16))
    ctx_count = lax.axis_size("ctx")
    piece_width = channels // ctx_count
    offset = lax.axis_index("ctx") * piece_width
    own_rates = lax.dynamic_slice_in_dim(decay_rates, offset, piece_width, 0)
    own_residues = lax.dynamic_slice_in_dim(residues, offset, piece_width, 0)
    block_len = math.gcd(seq_rows * ctx_count, 128)
    group_width = math.gcd(piece_width, 64)
    zero_state = jnp.zeros((piece_width, mode_count), jnp.float32)
    line_in = lax.all_to_all(gated, "ctx", split_axis=1, concat_axis=0, tiled=True).astype(
        jnp.float32
    )
    conv_line = from_groups(
        grouped(
            partial(forward_work, block_len=block_len),
            (line_in,),
            (own_rates, own_residues, zero_state),
            group_width,
        )
    )
    convolved = lax.all_to_all(
        conv_line.astype(jnp.bfloat16), "ctx", split_axis=0, concat_axis=1, tiled=True
    )
    line_back = lax.all_to_all(pulled, "ctx", split_axis=1, concat_axis=0, tiled=True).astype(
        jnp.float32
    )
    adj_line, raw_grad = grouped(
        partial(backward_work, block_len=block_len),
        (line_in, line_back),
        (own_rates, own_residues, zero_state, zero_state),
        group_width,
    )
    adjoint = lax.all_to_all(
        from_groups(adj_line).astype(jnp.bfloat16), "ctx", split_axis=0, concat_axis=1, tiled=True
    )
    own_raw = flat_table(raw_grad)
    mixed = convolved.astype(jnp.float32) + skip_gain[None, :] * gated.astype(jnp.float32)
    operator_out = (queries_f * mixed).astype(jnp.bfloat16)
    grad_queries = (cot_f * mixed).astype(jnp.bfloat16)
    grad_gated = adjoint.astype(jnp.float32) + skip_gain[None, :] * pulled.astype(jnp.float32)
    grad_keys = (grad_gated * values_f).astype(jnp.bfloat16)
    grad_values = (grad_gated * keys_f).astype(jnp.bfloat16)
    raw_all = lax.all_gather(own_raw, "ctx", axis=0, tiled=True)
    grad_square = lax.psum(jnp.sum(raw_all * raw_all), "tp")
    factor = jnp.minimum(1.0, math.sqrt(D * ORDER) / jnp.sqrt(grad_square + 1e-06))
    grad_residues = raw_all * factor
    return (operator_out, grad_queries, grad_keys, grad_values, grad_residues)


def solution(mesh):
    in_specs = (
        P("ctx", "tp"),
        P("ctx", "tp"),
        P("ctx", "tp"),
        P("tp", None),
        P("tp", None),
        P("tp"),
        P("ctx", "tp"),
    )
    out_specs = (P("ctx", "tp"), P("ctx", "tp"), P("ctx", "tp"), P("ctx", "tp"), P("tp", None))
    return jax.shard_map(shards, mesh=mesh, in_specs=in_specs, out_specs=out_specs, check_vma=False)
```

profile of v0, /device:TPU:32, one launch (start us, length us, event | category | flops | bytes accessed | tf_op | source)
XLA Modules:
  0.0 280.1 jit_solution(7708082309188066356)
XLA Ops:
  3.5 15.9 %all-to-all-start = ((bf16[128,32,16]{0,2,1:T(8,128)(2,1)}), bf16[128,32,16]{0,2,1:T(8,128)(2,1)}, u32[]{:S(2)}, u32[]{:S(2)}) async-start(bf16[128,32,16]{0,2,1:T(8,128)(2,1)} %bitcast.8), calls=%async_computation | async-start | bytes 262144 | tf_op jit(solution)/shard_map/all_to_all | solution.py:131
  20.7 1.3 fusion.56
  24.3 54.4 %gather_fusion = f32[16384,16]{1,0:T(8,128)} fusion(f32[128,16]{1,0:T(8,128)S(1)} %bitcast.55, s32[16384]{0:T(1024)S(1)} %bitcast_clamp_fusion), kind=kCustom, calls=%fused_computation | custom fusion | bytes 2162688 | tf_op jit(solution)/shard_map/while/body/eval_jaxpr/gather | solution.py:27
  78.7 6.8 %copy.139 = f32[128,128,16]{0,1,2:T(8,128)S(1)} copy(f32[128,128,16]{2,1,0:T(8,128)} %bitcast.56) | data formatting | bytes 2097152 | tf_op jit(solution)/shard_map/while/body/eval_jaxpr/gather | solution.py:27
  86.2 2.2 fusion.10
  97.1 1.5 fusion.14
  98.6 2.0 fusion.4
  101.4 12.2 %all-to-all-start.1 = ((bf16[32,128,16]{1,2,0:T(8,128)(2,1)}), bf16[32,128,16]{1,2,0:T(8,128)(2,1)S(1)}, u32[]{:S(2)}, u32[]{:S(2)}) async-start(bf16[32,128,16]{1,2,0:T(8,128)(2,1)} %copy.149), calls=%async_computation.1 | async-start | bytes 262144 | tf_op jit(solution)/shard_map/all_to_all | solution.py:142
  115.4 6.9 %all-to-all-done.1 = bf16[32,128,16]{1,2,0:T(8,128)(2,1)S(1)} async-done(((bf16[32,128,16]{1,2,0:T(8,128)(2,1)}), bf16[32,128,16]{1,2,0:T(8,128)(2,1)S(1)}, u32[]{:S(2)}, u32[]{:S(2)}) %all-to-all-start.1) | async-done | bytes 131104 | tf_op jit(solution)/shard_map/all_to_all | solution.py:142
  122.3 1.9 fusion.24
  124.2 8.2 %all-to-all-start.2 = ((bf16[128,32,16]{0,2,1:T(8,128)(2,1)}), bf16[128,32,16]{0,2,1:T(8,128)(2,1)S(1)}, u32[]{:S(2)}, u32[]{:S(2)}) async-start(bf16[128,32,16]{0,2,1:T(8,128)(2,1)} %bitcast.63), calls=%async_computation.2 | async-start | bytes 262144 | tf_op jit(solution)/shard_map/all_to_all | solution.py:145
  134.1 1.7 copy.178
  135.9 1.7 copy.165
  137.6 3.6 %all-to-all-done.2 = bf16[128,32,16]{0,2,1:T(8,128)(2,1)S(1)} async-done(((bf16[128,32,16]{0,2,1:T(8,128)(2,1)}), bf16[128,32,16]{0,2,1:T(8,128)(2,1)S(1)}, u32[]{:S(2)}, u32[]{:S(2)}) %all-to-all-start.2) | async-done | bytes 131104 | tf_op jit(solution)/shard_map/all_to_all | solution.py:145
  142.1 1.7 copy.155
  147.5 1.9 pad.116
  149.4 1.9 pad.117
  151.3 1.4 add.275
  152.7 1.4 fusion.41
  154.1 1.3 slice.495
  155.4 1.4 pad.119
  156.8 1.4 pad_maximum_fusion.5
  158.1 3.2 %pad.118 = f32[8,16,16]{2,1,0:T(8,128)} pad(f32[4,16,16]{2,1,0:T(8,128)} %pad_maximum_fusion.5, f32[]{:T(128)} %constant.76.clone.1), padding=0_1_1x0_0_0x0_0_0 | pad | bytes 12292 | tf_op jit(solution)/shard_map/while/body/eval_jaxpr/pad | solution.py:46
  162.3 1.5 add.277
  163.8 1.6 slice.469
  166.0 1.3 fusion
  167.3 1.8 fusion.6
  169.2 1.1 fusion.5
  170.3 51.1 %all_gather.3 = f32[512,16]{1,0:T(8,128)S(1)} all-gather(f32[16,16]{1,0:T(8,128)S(1)} %add_multiply_fusion.6), channel_id=1, replica_groups=mesh['ctx'=32,'tp'=16] {'ctx'}, dimensions={0}, use_global_device_ids=true | all-gather | bytes 33792 | tf_op jit(solution)/shard_map/all_gather | solution.py:164
  223.6 2.0 fusion.3
  226.3 7.4 %all-to-all-start.3 = ((bf16[32,128,16]{1,2,0:T(8,128)(2,1)}), bf16[32,128,16]{1,2,0:T(8,128)(2,1)S(1)}, u32[]{:S(2)}, u32[]{:S(2)}) async-start(bf16[32,128,16]{1,2,0:T(8,128)(2,1)} %copy.158), calls=%async_computation.3 | async-start | bytes 262144 | tf_op jit(solution)/shard_map/all_to_all | solution.py:154
  235.2 41.7 %psum.7 = f32[]{:T(128)} all-reduce(f32[]{:T(128)} %multiply_reduce_fusion), channel_id=1, replica_groups=mesh['ctx'=32,'tp'=16] {'tp'}, use_global_device_ids=true, to_apply=%region_1.2 | all-reduce | flops 1 | bytes 8 | tf_op jit(solution)/shard_map/psum | solution.py:165
  (146 shorter events, 32.5 us)
Async XLA Ops:
  0.6 18.8 %copy-start = (f32[512,16]{0,1:T(8,128)S(1)}, f32[512,16]{0,1:T(8,128)}, u32[]{:S(2)}) copy-start(f32[512,16]{0,1:T(8,128)} %param.10) | copy-start | bytes 98308
  1.7 19.0 %copy-start.2 = (bf16[128,512]{0,1:T(8,128)(2,1)}, bf16[128,512]{0,1:T(8,128)(2,1)S(1)}, u32[]{:S(2)}) copy-start(bf16[128,512]{0,1:T(8,128)(2,1)S(1)} %copy.140) | copy-start | bytes 393220
  2.8 17.9 %copy-start.4 = (bf16[128,512]{0,1:T(8,128)(2,1)}, bf16[128,512]{0,1:T(8,128)(2,1)S(1)}, u32[]{:S(2)}) copy-start(bf16[128,512]{0,1:T(8,128)(2,1)S(1)} %copy.141) | copy-start | bytes 393220
  3.5 82.7 %all-to-all-start = ((bf16[128,32,16]{0,2,1:T(8,128)(2,1)}), bf16[128,32,16]{0,2,1:T(8,128)(2,1)}, u32[]{:S(2)}, u32[]{:S(2)}) async-start(bf16[128,32,16]{0,2,1:T(8,128)(2,1)} %bitcast.8), calls=%async_computation | async-start | bytes 262144 | tf_op jit(solution)/shard_map/all_to_all | solution.py:131
  19.6 0.9 copy-start.15
  94.1 2.0 copy-start.23
  96.3 2.3 copy-start.1
  98.6 15.0 %copy-start.17 = (bf16[128,512]{1,0:T(8,128)(2,1)S(1)}, bf16[128,512]{1,0:T(8,128)(2,1)}, u32[]{:S(2)}) copy-start(bf16[128,512]{1,0:T(8,128)(2,1)} %param.7) | copy-start | bytes 393220
  98.6 15.8 %copy-start.18 = (bf16[128,512]{1,0:T(8,128)(2,1)S(1)}, bf16[128,512]{1,0:T(8,128)(2,1)}, u32[]{:S(2)}) copy-start(bf16[128,512]{1,0:T(8,128)(2,1)} %param.13) | copy-start | bytes 393220
  98.6 16.6 %copy-start.16 = (f32[16,16]{1,0:T(8,128)S(1)}, f32[16,16]{1,0:T(8,128)}, u32[]{:S(2)}) copy-start(f32[16,16]{1,0:T(8,128)} %copy-done.15) | copy-start | bytes 3076
  100.7 21.6 %copy-start.20 = (f32[512]{0:T(512)S(1)}, f32[512]{0:T(512)}, u32[]{:S(2)}) copy-start(f32[512]{0:T(512)} %param.12) | copy-start | bytes 6148
  101.4 20.9 %all-to-all-start.1 = ((bf16[32,128,16]{1,2,0:T(8,128)(2,1)}), bf16[32,128,16]{1,2,0:T(8,128)(2,1)S(1)}, u32[]{:S(2)}, u32[]{:S(2)}) async-start(bf16[32,128,16]{1,2,0:T(8,128)(2,1)} %copy.149), calls=%async_computation.1 | async-start | bytes 262144 | tf_op jit(solution)/shard_map/all_to_all | solution.py:142
  124.2 16.9 %all-to-all-start.2 = ((bf16[128,32,16]{0,2,1:T(8,128)(2,1)}), bf16[128,32,16]{0,2,1:T(8,128)(2,1)S(1)}, u32[]{:S(2)}, u32[]{:S(2)}) async-start(bf16[128,32,16]{0,2,1:T(8,128)(2,1)} %bitcast.63), calls=%async_computation.2 | async-start | bytes 262144 | tf_op jit(solution)/shard_map/all_to_all | solution.py:145
  144.9 0.7 copy-start.7
  144.9 0.7 copy-start.8
  145.6 0.6 copy-start.13
  161.3 6.0 %copy-start.9 = (f32[16,16,128]{2,1,0:T(8,128)S(1)}, f32[16,16,128]{2,1,0:T(8,128)}, u32[]{:S(2)}) copy-start(f32[16,16,128]{2,1,0:T(8,128)} %copy.184) | copy-start | bytes 393220
  166.0 3.1 %copy-start.10 = (f32[16,16,32]{2,1,0:T(8,128)S(1)}, f32[16,16,32]{2,1,0:T(8,128)}, u32[]{:S(2)}) copy-start(f32[16,16,32]{2,1,0:T(8,128)} %copy.178) | copy-start | bytes 98308
  169.1 52.2 %copy-start.19 = (f32[1,16,16]{2,1,0:T(8,128)S(1)}, f32[1,16,16]{2,1,0:T(8,128)}, u32[]{:S(2)}) copy-start(f32[1,16,16]{2,1,0:T(8,128)} %slice.495) | copy-start | bytes 3076
  169.2 52.3 %copy-start.14 = (f32[8,16,16]{2,1,0:T(8,128)S(1)}, f32[8,16,16]{2,1,0:T(8,128)}, u32[]{:S(2)}) copy-start(f32[8,16,16]{2,1,0:T(8,128)} %add.277) | copy-start | bytes 24580
  170.3 51.4 %copy-start.12 = (f32[15,16,16]{2,1,0:T(8,128)S(1)}, f32[15,16,16]{2,1,0:T(8,128)}, u32[]{:S(2)}) copy-start(f32[15,16,16]{2,1,0:T(8,128)} %slice.469) | copy-start | bytes 46084
  221.8 0.6 copy-start.22
  223.6 10.8 %copy-start.11 = (bf16[128,512]{0,1:T(8,128)(2,1)S(1)}, bf16[128,512]{0,1:T(8,128)(2,1)}, u32[]{:S(2)}) copy-start(bf16[128,512]{0,1:T(8,128)(2,1)} %get-tuple-element.74) | copy-start | bytes 393220
  225.6 52.8 %copy-start.3 = (bf16[128,512]{0,1:T(8,128)(2,1)S(1)}, bf16[128,512]{0,1:T(8,128)(2,1)}, u32[]{:S(2)}) copy-start(bf16[128,512]{0,1:T(8,128)(2,1)} %copy-done.2) | copy-start | bytes 393220
  225.6 52.8 %copy-start.5 = (bf16[128,512]{0,1:T(8,128)(2,1)S(1)}, bf16[128,512]{0,1:T(8,128)(2,1)}, u32[]{:S(2)}) copy-start(bf16[128,512]{0,1:T(8,128)(2,1)} %copy-done.4) | copy-start | bytes 393220
  225.6 52.7 %copy-start.6 = (bf16[128,512]{0,1:T(8,128)(2,1)S(1)}, bf16[128,512]{0,1:T(8,128)(2,1)}, u32[]{:S(2)}) copy-start(bf16[128,512]{0,1:T(8,128)(2,1)} %get-tuple-element.76) | copy-start | bytes 393220
  225.6 52.7 %copy-start.21 = (f32[512]{0:T(512)S(1)}, f32[512]{0:T(512)}, u32[]{:S(2)}) copy-start(f32[512]{0:T(512)} %param.12) | copy-start | bytes 6148
  226.3 52.0 %all-to-all-start.3 = ((bf16[32,128,16]{1,2,0:T(8,128)(2,1)}), bf16[32,128,16]{1,2,0:T(8,128)(2,1)S(1)}, u32[]{:S(2)}, u32[]{:S(2)}) async-start(bf16[32,128,16]{1,2,0:T(8,128)(2,1)} %copy.158), calls=%async_computation.3 | async-start | bytes 262144 | tf_op jit(solution)/shard_map/all_to_all | solution.py:154
where the time goes:
time: 282 us; the launch traced here: 280 us
  local copies, waits for them, and re-layouts  96.8 us (34%)
  blocking collectives  92.8 us (33%)
  starting transfers between devices  43.7 us (15%)
  other arithmetic  20.1 us (7%)
  matrix products  14.2 us (5%)
  waiting for transfers between devices  10.5 us (4%)
    gather x2, local copies, waits for them, and re-layouts, prepare(): short_filter[jnp.maximum(lag_table, 0)]  61.2 us
    all_gather x1, blocking collectives, shards(): raw_all = lax.all_gather(own_raw, 'ctx', axis=0, tiled=True)  51.1 us
    psum x1, blocking collectives, shards(): grad_square = lax.psum(jnp.sum(raw_all * raw_all), 'tp')  41.7 us
    all_to_all x1, starting transfers between devices, shards(): lax.all_to_all(gated, 'ctx', split_axis=1, concat_axis=0, tiled=True)  15.9 us
    unnamed x64, local copies, waits for them, and re-layouts  14 us
    all_to_all x1, starting transfers between devices, shards(): lax.all_to_all(conv_line.astype(jnp.bfloat16), 'ctx', split_axis=0, conca...  12.2 us
    pad x8, local copies, waits for them, and re-layouts, backward_states(): lax.associative_scan(chain_link, (decays[::-1], start_states[::-1]), axis=0)  8.84 us
    all_to_all x1, starting transfers between devices, shards(): lax.all_to_all(pulled, 'ctx', split_axis=1, concat_axis=0, tiled=True)  8.18 us
  transfers between devices with their start and end apart: 4, of which 2 were waited for; matrix products, arithmetic and copies ran while one was open for 27% of the time, Pallas kernels for 0%

commit v1 on v0

v1 whole, which is shorter than its diff:
```python
import math

import jax
import jax.numpy as jnp
from jax import lax
from jax.experimental import pallas as pl
from jax.experimental.pallas import tpu as pltpu
from jax.sharding import PartitionSpec as P

D = 8192
ORDER = 16
LANES = 128
ROWS = 8
SEG = 16
NSEG = 8
CTX = 32
MESH = pl.DeviceIdType.MESH


def kernel(
    q_hbm, k_hbm, v_hbm, c_hbm, dec_hbm, res_hbm, skip_hbm,
    op_hbm, gq_hbm, gk_hbm, gv_hbm, gr_hbm,
    q_in, k_in, v_in, c_in, dec, res, skip,
    op_out, gq_out, gk_out, gv_out, gr_out,
    xs, ps, hs, gs, far, pw, taps, yl, zl, yn, zn, dt,
    send1, recv1, send2, recv2, part,
    in_sems, out_sems, send_sems, recv_sems,
):
    me, mt = lax.axis_index("ctx"), lax.axis_index("tp")
    n_tp = part.shape[0]
    rows, chans = q_in.shape
    cts = chans // LANES

    ins = [
        pltpu.make_async_copy(src, dst, in_sems.at[i])
        for i, (src, dst) in enumerate(
            zip((dec_hbm, res_hbm, skip_hbm, k_hbm, v_hbm, q_hbm, c_hbm), (dec, res, skip, k_in, v_in, q_in, c_in))
        )
    ]
    for copy in ins[3:] + ins[:3]:
        copy.start()

    barrier = pltpu.get_barrier_semaphore()

    @pl.loop(1, CTX)
    def _(off):
        pl.semaphore_signal(barrier, inc=1, device_id={"ctx": lax.rem(me + off, CTX)}, device_id_type=MESH)

    @pl.loop(1, n_tp)
    def _(off):
        pl.semaphore_signal(barrier, inc=1, device_id={"tp": lax.rem(mt + off, n_tp)}, device_id_type=MESH)

    def lanes(ct):
        return pl.ds(ct * LANES, LANES)

    for copy in ins:
        copy.wait()

    for ct in range(cts):
        for r in range(rows // 16):
            at = (pl.ds(r * 16, 16), lanes(ct))
            to = pl.ds(ct * rows + r * 16, 16)
            kv = k_in[at].astype(jnp.float32) * v_in[at].astype(jnp.float32)
            cq = c_in[at].astype(jnp.float32) * q_in[at].astype(jnp.float32)
            xs[to, :] = kv.astype(jnp.bfloat16).astype(jnp.float32)
            ps[to, :] = cq.astype(jnp.bfloat16).astype(jnp.float32)

    pieces = [(half, ct) for half in range(2) for ct in range(cts)]
    rate = [dec[pl.ds(half * ROWS, ROWS), lanes(ct)] for half, ct in pieces]
    decay = [jnp.exp(-d) for d in rate]

    for (half, ct), d in zip(pieces, rate):
        for pair in range(4):
            dt[pl.ds(ct * 64 + 2 * pair + half, ROWS, stride=ROWS), :] = d

    def wide(ref, row):
        return jnp.broadcast_to(ref[pl.ds(row, 1), :], (ROWS, LANES))

    zeros = [jnp.zeros((ROWS, LANES), jnp.float32) for _ in pieces]

    def scan_segment(r, state):
        fwd, inner, bwd = (list(part_) for part_ in state)
        back = NSEG - 1 - r
        for j, (half, ct) in enumerate(pieces):
            hs[pl.ds(pl.multiple_of(ct * rows + r * SEG + half * ROWS, ROWS), ROWS), :] = fwd[j]
            gs[pl.ds(pl.multiple_of(ct * rows + back * SEG + half * ROWS, ROWS), ROWS), :] = bwd[j]
        for i in range(SEG):
            for ct in range(cts):
                x = wide(xs, ct * rows + r * SEG + i)
                p = wide(ps, ct * rows + r * SEG + i)
                pb = wide(ps, ct * rows + back * SEG + (SEG - 1 - i))
                for half in range(2):
                    j = half * cts + ct
                    fwd[j] = fwd[j] * decay[j] + x
                    inner[j] = inner[j] + fwd[j] * p
                    bwd[j] = bwd[j] * decay[j] + pb
        return fwd, inner, bwd

    fwd, inner, bwd = lax.fori_loop(0, NSEG, scan_segment, (zeros, zeros, zeros))

    for j, (half, ct) in enumerate(pieces):
        for pair, value in enumerate((fwd[j], bwd[j], inner[j], zeros[j])):
            send1[pl.ds(ct * 64 + 2 * pair + half, ROWS, stride=ROWS), :] = value

    def tile(index):
        return pl.ds(pl.multiple_of(index * ROWS, ROWS), ROWS)

    pl.semaphore_wait(barrier, CTX - 1 + n_tp - 1)

    def exchange(src, dst, which):
        @pl.loop(1, CTX)
        def _(off):
            to = lax.rem(me + off, CTX)
            pltpu.make_async_remote_copy(
                src_ref=src.at[tile(to), :],
                dst_ref=dst.at[tile(me), :],
                send_sem=send_sems.at[which],
                recv_sem=recv_sems.at[which],
                device_id={"ctx": to},
                device_id_type=MESH,
            ).start()

    def arrived(dst, sem):
        most = dst.at[pl.ds(0, (CTX - 1) * ROWS), :]
        pltpu.make_async_copy(most, most, sem).wait()

    exchange(send1, recv1, 0)
    recv1[tile(me), :] = send1[tile(me), :]

    unit = [jnp.sqrt(1.0 - jnp.exp(-2.0 * d)) for d in rate]
    coef = [
        res[pl.ds(half * ROWS, ROWS), lanes(ct)] * unit[j] for j, (half, ct) in enumerate(pieces)
    ]

    @pl.loop(0, SEG + 1)
    def _(i):
        lag = i.astype(jnp.float32)
        for ct in range(cts):
            total = None
            for half in range(2):
                j = half * cts + ct
                power = coef[j] * jnp.exp(-rate[j] * lag)
                pw[pl.ds(pl.multiple_of((ct * (SEG + 1) + i) * ORDER + half * ROWS, ROWS), ROWS), :] = power
                total = power if total is None else total + power
            total = jnp.sum(total, axis=0, keepdims=True)
            taps[tile(ct * (SEG + 1) + i), :] = jnp.broadcast_to(total, (ROWS, LANES))

    @pl.loop(0, NSEG)
    def _(r):
        lag = (r * SEG).astype(jnp.float32)
        for j, (half, ct) in enumerate(pieces):
            far[pl.ds(pl.multiple_of(ct * rows + r * SEG + half * ROWS, ROWS), ROWS), :] = jnp.exp(-rate[j] * lag)

    @pl.loop(0, cts)
    def _(ct):
        x = [xs[pl.ds(ct * rows + i, NSEG, stride=SEG), :] for i in range(SEG)]
        p = [ps[pl.ds(ct * rows + i, NSEG, stride=SEG), :] for i in range(SEG)]
        tap = [taps[tile(ct * (SEG + 1) + i), :] for i in range(SEG)]
        for i in range(SEG):
            y = x[i] * tap[0]
            for lag in range(1, i + 1):
                y = y + x[i - lag] * tap[lag]
            yl[tile(ct * SEG + i), :] = y
            z = p[i] * tap[0]
            for lag in range(1, SEG - i):
                z = z + p[i + lag] * tap[lag]
            zl[tile(ct * SEG + i), :] = z

    mine = dt[tile(me), :]
    block = jnp.exp(-float(rows) * mine)
    step = jnp.exp(-mine)
    line = lax.broadcasted_iota(jnp.int32, (ROWS, LANES), 0)
    zero = jnp.zeros((ROWS, LANES), jnp.float32)
    arrived(recv1, recv_sems.at[0])

    carry, cross, inside = zero, zero, zero
    for e in range(CTX):
        got = recv1[pl.ds(e * ROWS, ROWS), :]
        send2[pl.ds(e * ROWS, ROWS), :] = carry
        cross = cross + pltpu.roll(got, ROWS - 2, 0) * carry
        inside = inside + got
        carry = carry * block + got
    raw_tile = inside + pltpu.roll(step * cross, 4, 0)
    carry = zero
    for e in reversed(range(CTX)):
        got = recv1[pl.ds(e * ROWS, ROWS), :]
        before = send2[pl.ds(e * ROWS, ROWS), :]
        send2[pl.ds(e * ROWS, ROWS), :] = jnp.where(line < 2, before, jnp.where(line < 4, carry, raw_tile))
        carry = carry * block + got

    exchange(send2, recv2, 1)
    recv2[tile(me), :] = send2[tile(me), :]
    arrived(recv2, recv_sems.at[1])

    def from_owners(pair, half, ct):
        return recv2[pl.ds(ct * 64 + 2 * pair + half, ROWS, stride=ROWS), :]

    raw = [unit[j] * from_owners(2, half, ct) for j, (half, ct) in enumerate(pieces)]
    square = raw[0] * raw[0]
    for value in raw[1:]:
        square = square + value * value
    part[mt] = jnp.sum(square, axis=0, keepdims=True)

    @pl.loop(1, n_tp)
    def _(off):
        pltpu.make_async_remote_copy(
            src_ref=part.at[mt],
            dst_ref=part.at[mt],
            send_sem=send_sems.at[2],
            recv_sem=recv_sems.at[2],
            device_id={"tp": lax.rem(mt + off, n_tp)},
            device_id_type=MESH,
        ).start()

    before = [from_owners(0, half, ct) for half, ct in pieces]
    after = [from_owners(1, half, ct) for half, ct in pieces]

    @pl.loop(0, NSEG)
    def _(r):
        for j, (half, ct) in enumerate(pieces):
            here = pl.ds(pl.multiple_of(ct * rows + r * SEG + half * ROWS, ROWS), ROWS)
            there = pl.ds(pl.multiple_of(ct * rows + (NSEG - 1 - r) * SEG + half * ROWS, ROWS), ROWS)
            hs[here, :] = hs[here, :] + far[here, :] * before[j]
            gs[here, :] = gs[here, :] + far[there, :] * after[j]

    def out_copies(at):
        return [
            pltpu.make_async_copy(src.at[at], dst.at[at], out_sems.at[i])
            for i, (src, dst) in enumerate(
                ((op_out, op_hbm), (gq_out, gq_hbm), (gk_out, gk_hbm), (gv_out, gv_hbm))
            )
        ]

    @pl.loop(0, cts)
    def _(ct):
        h = [hs[pl.ds(ct * rows + n, NSEG, stride=SEG), :] for n in range(ORDER)]
        g = [gs[pl.ds(ct * rows + n, NSEG, stride=SEG), :] for n in range(ORDER)]
        for i in range(SEG):
            y = yl[tile(ct * SEG + i), :]
            z = zl[tile(ct * SEG + SEG - 1 - i), :]
            ys, zs = [], []
            for n in range(ORDER):
                power = wide(pw, (ct * (SEG + 1) + i + 1) * ORDER + n)
                ys.append(power * h[n])
                zs.append(power * g[n])
            while len(ys) > 1:
                ys = [a + b for a, b in zip(ys[::2], ys[1::2])]
                zs = [a + b for a, b in zip(zs[::2], zs[1::2])]
            yn[pl.ds(ct * rows + i, NSEG, stride=SEG), :] = y + ys[0]
            zn[pl.ds(ct * rows + SEG - 1 - i, NSEG, stride=SEG), :] = z + zs[0]
        cols = pl.ds(pl.multiple_of(ct * LANES, LANES), LANES)
        gain = jnp.broadcast_to(skip[:, cols], (SEG, LANES))
        for r in range(rows // SEG):
            at = (pl.ds(r * SEG, SEG), cols)
            here = pl.ds(pl.multiple_of(ct * rows + r * SEG, SEG), SEG)
            conv = yn[here, :].astype(jnp.bfloat16).astype(jnp.float32)
            adj = zn[here, :].astype(jnp.bfloat16).astype(jnp.float32)
            mixed = conv + gain * xs[here, :]
            grad = adj + gain * ps[here, :]
            op_out[at] = (q_in[at].astype(jnp.float32) * mixed).astype(jnp.bfloat16)
            gq_out[at] = (c_in[at].astype(jnp.float32) * mixed).astype(jnp.bfloat16)
            gk_out[at] = (v_in[at].astype(jnp.float32) * grad).astype(jnp.bfloat16)
            gv_out[at] = (k_in[at].astype(jnp.float32) * grad).astype(jnp.bfloat16)
        for copy in out_copies((slice(None), cols)):
            copy.start()

    others = part.at[pl.ds(0, n_tp - 1)]
    pltpu.make_async_copy(others, others, recv_sems.at[2]).wait()
    total = jnp.sum(jnp.sum(part[...], axis=0), axis=1, keepdims=True)
    factor = jnp.minimum(1.0, math.sqrt(D * ORDER) / jnp.sqrt(total + 1e-06))
    for j, (half, ct) in enumerate(pieces):
        gr_out[pl.ds(half * ROWS, ROWS), lanes(ct)] = raw[j] * factor
    last = pltpu.make_async_copy(gr_out, gr_hbm, out_sems.at[4])
    last.start()
    arrived(send1, send_sems.at[0])
    arrived(send2, send_sems.at[1])
    pltpu.make_async_copy(others, others, send_sems.at[2]).wait()
    for copy in out_copies((slice(None), slice(None))):
        copy.wait()
    last.wait()


def shards(queries, keys_in, values_in, decay_rates, residues, skip_gain, cotangent):
    rows, chans = queries.shape
    n_tp = lax.axis_size("tp")
    cts = chans // LANES
    f32, bf16 = jnp.float32, jnp.bfloat16
    line = jax.ShapeDtypeStruct((rows, chans), bf16)
    anywhere = pl.BlockSpec(memory_space=pl.ANY)
    table = pltpu.VMEM((cts * rows, LANES), f32)
    posts = pltpu.VMEM((CTX * ROWS, LANES), f32)
    outs = pl.pallas_call(
        kernel,
        out_shape=(line, line, line, line, jax.ShapeDtypeStruct((ORDER, chans), f32)),
        in_specs=[anywhere] * 7,
        out_specs=(anywhere,) * 5,
        scratch_shapes=[
            *[pltpu.VMEM((rows, chans), bf16)] * 4,
            pltpu.VMEM((ORDER, chans), f32),
            pltpu.VMEM((ORDER, chans), f32),
            pltpu.VMEM((1, chans), f32),
            *[pltpu.VMEM((rows, chans), bf16)] * 4,
            pltpu.VMEM((ORDER, chans), f32),
            *[table] * 5,
            pltpu.VMEM((cts * (SEG + 1) * ORDER, LANES), f32),
            pltpu.VMEM((cts * (SEG + 1) * ROWS, LANES), f32),
            *[table] * 4,
            posts,
            *[posts] * 4,
            pltpu.VMEM((n_tp, 1, LANES), f32),
            pltpu.SemaphoreType.DMA((7,)),
            pltpu.SemaphoreType.DMA((5,)),
            pltpu.SemaphoreType.DMA((3,)),
            pltpu.SemaphoreType.DMA((3,)),
        ],
        compiler_params=pltpu.CompilerParams(collective_id=0, has_side_effects=True, vmem_limit_bytes=32 * 2**20),
        name="modal_conv",
    )(queries, keys_in, values_in, cotangent, decay_rates.T, residues.T, skip_gain.reshape(1, chans))
    return (*outs[:4], outs[4].T)


def solution(mesh):
    line, modes = P("ctx", "tp"), P("tp", None)
    in_specs = (line, line, line, modes, modes, P("tp"), line)
    out_specs = (line, line, line, line, modes)
    return jax.shard_map(shards, mesh=mesh, in_specs=in_specs, out_specs=out_specs, check_vma=False)
```

time: 282 us -> 48.2 us (0.17)
  the two profiles are of different devices: /device:TPU:32 before, /device:TPU:1 now
where the time goes in v1:
time: 48.2 us; the launch traced here: 47.8 us
  Pallas kernels  38.1 us (79%)
  local copies, waits for them, and re-layouts  9.04 us (19%)
  between operations  0.66 us (1%)
    pallas_call x1, Pallas kernels, shards(): pl.pallas_call(kernel, out_shape=(line, line, line, line, jax.ShapeDtypeS...  38.1 us
    unnamed x19, local copies, waits for them, and re-layouts  9.04 us

profile of v1, /device:TPU:1, one launch (start us, length us, event | category | flops | bytes accessed | tf_op | source)
XLA Modules:
  0.0 47.8 jit_solution(14691512800850139827)
XLA Ops:
  0.6 0.0 copy-start.6
  0.6 0.7 %copy-done.6 = f32[512]{0:T(512)S(1)} copy-done((f32[512]{0:T(512)S(1)}, f32[512]{0:T(512)}, u32[]{:S(2)}) %copy-start.6) | copy-done | bytes 2072
  1.3 0.0 copy-start
  1.3 0.9 %copy-done = bf16[128,512]{1,0:T(8,128)(2,1)S(1)} copy-done((bf16[128,512]{1,0:T(8,128)(2,1)S(1)}, bf16[128,512]{1,0:T(8,128)(2,1)}, u32[]{:S(2)}) %copy-start) | copy-done | bytes 131096
  2.2 0.0 copy-start.1
  2.2 0.9 %copy-done.1 = bf16[128,512]{1,0:T(8,128)(2,1)S(1)} copy-done((bf16[128,512]{1,0:T(8,128)(2,1)S(1)}, bf16[128,512]{1,0:T(8,128)(2,1)}, u32[]{:S(2)}) %copy-start.1) | copy-done | bytes 131096
  3.1 0.0 copy-start.2
  3.1 0.9 %copy-done.2 = bf16[128,512]{1,0:T(8,128)(2,1)S(1)} copy-done((bf16[128,512]{1,0:T(8,128)(2,1)S(1)}, bf16[128,512]{1,0:T(8,128)(2,1)}, u32[]{:S(2)}) %copy-start.2) | copy-done | bytes 131096
  4.0 0.0 copy-start.3
  4.0 0.9 %copy-done.3 = bf16[128,512]{1,0:T(8,128)(2,1)S(1)} copy-done((bf16[128,512]{1,0:T(8,128)(2,1)S(1)}, bf16[128,512]{1,0:T(8,128)(2,1)}, u32[]{:S(2)}) %copy-start.3) | copy-done | bytes 131096
  4.9 0.0 copy-start.4
  4.9 0.8 %copy-done.4 = f32[512,16]{0,1:T(8,128)S(1)} copy-done((f32[512,16]{0,1:T(8,128)S(1)}, f32[512,16]{0,1:T(8,128)}, u32[]{:S(2)}) %copy-start.4) | copy-done | bytes 32792
  5.7 0.0 copy-start.5
  5.7 0.8 %copy-done.5 = f32[512,16]{0,1:T(8,128)S(1)} copy-done((f32[512,16]{0,1:T(8,128)S(1)}, f32[512,16]{0,1:T(8,128)}, u32[]{:S(2)}) %copy-start.5) | copy-done | bytes 32792
  6.5 38.1 %modal_conv.1 = (bf16[128,512]{1,0:T(8,128)(2,1)S(1)}, bf16[128,512]{1,0:T(8,128)(2,1)S(1)}, bf16[128,512]{1,0:T(8,128)(2,1)S(1)}, bf16[128,512]{1,0:T(8,128)(2,1)S(1)}, f32[16,512]{1,0:T(8,128)S(1)}) custom-call(bf16[128,512]{1,0:T(8,128)(2,1)S(1)} %copy-done, bf16[128,512]{1,0:T(8,128)(2,1)S(1)} %copy-done.1, bf16[128,512]{1,0:T(8,128)(2,1)S(1)} %copy-done.2, ...), custom_call_target="tpu_custom_call" | custom-call | tf_op jit(solution)/shard_map/modal_conv/pallas_call | solution.py:292
  44.6 0.7 %copy.17 = bf16[128,512]{1,0:T(8,128)(2,1)} copy(bf16[128,512]{1,0:T(8,128)(2,1)S(1)} %get-tuple-element.20) | data formatting | bytes 262144
  45.2 0.7 %copy.18 = bf16[128,512]{1,0:T(8,128)(2,1)} copy(bf16[128,512]{1,0:T(8,128)(2,1)S(1)} %get-tuple-element.21) | data formatting | bytes 262144
  45.9 0.7 %copy.19 = bf16[128,512]{1,0:T(8,128)(2,1)} copy(bf16[128,512]{1,0:T(8,128)(2,1)S(1)} %get-tuple-element.22) | data formatting | bytes 262144
  46.6 0.7 %copy.20 = bf16[128,512]{1,0:T(8,128)(2,1)} copy(bf16[128,512]{1,0:T(8,128)(2,1)S(1)} %get-tuple-element.23) | data formatting | bytes 262144
  47.2 0.6 %copy.21 = f32[512,16]{0,1:T(8,128)} copy(f32[512,16]{0,1:T(8,128)S(1)} %bitcast.6) | data formatting | bytes 65536
Async XLA Ops:
  0.6 0.7 %copy-start.6 = (f32[512]{0:T(512)S(1)}, f32[512]{0:T(512)}, u32[]{:S(2)}) copy-start(f32[512]{0:T(512)} %param.12) | copy-start | bytes 6148
  1.3 0.9 %copy-start = (bf16[128,512]{1,0:T(8,128)(2,1)S(1)}, bf16[128,512]{1,0:T(8,128)(2,1)}, u32[]{:S(2)}) copy-start(bf16[128,512]{1,0:T(8,128)(2,1)} %q_hbm.1) | copy-start | bytes 393220
  2.2 0.9 %copy-start.1 = (bf16[128,512]{1,0:T(8,128)(2,1)S(1)}, bf16[128,512]{1,0:T(8,128)(2,1)}, u32[]{:S(2)}) copy-start(bf16[128,512]{1,0:T(8,128)(2,1)} %k_hbm.1) | copy-start | bytes 393220
  3.1 0.9 %copy-start.2 = (bf16[128,512]{1,0:T(8,128)(2,1)S(1)}, bf16[128,512]{1,0:T(8,128)(2,1)}, u32[]{:S(2)}) copy-start(bf16[128,512]{1,0:T(8,128)(2,1)} %v_hbm.1) | copy-start | bytes 393220
  4.0 0.9 %copy-start.3 = (bf16[128,512]{1,0:T(8,128)(2,1)S(1)}, bf16[128,512]{1,0:T(8,128)(2,1)}, u32[]{:S(2)}) copy-start(bf16[128,512]{1,0:T(8,128)(2,1)} %c_hbm.1) | copy-start | bytes 393220
  4.9 0.8 %copy-start.4 = (f32[512,16]{0,1:T(8,128)S(1)}, f32[512,16]{0,1:T(8,128)}, u32[]{:S(2)}) copy-start(f32[512,16]{0,1:T(8,128)} %param.10) | copy-start | bytes 98308
  5.7 0.8 %copy-start.5 = (f32[512,16]{0,1:T(8,128)S(1)}, f32[512,16]{0,1:T(8,128)}, u32[]{:S(2)}) copy-start(f32[512,16]{0,1:T(8,128)} %param.11) | copy-start | bytes 98308

commit v2 on v1

--- a/solution.py
+++ b/solution.py
@@ -14,6 +14,8 @@
 SEG = 16
 NSEG = 8
 CTX = 32
+OWNERS = 16
+PIECES = 2
 MESH = pl.DeviceIdType.MESH
 
 
@@ -22,12 +24,17 @@
     op_hbm, gq_hbm, gk_hbm, gv_hbm, gr_hbm,
     q_in, k_in, v_in, c_in, dec, res, skip,
     op_out, gq_out, gk_out, gv_out, gr_out,
-    xs, ps, hs, gs, far, pw, taps, yl, zl, yn, zn, dt,
-    send1, recv1, send2, recv2, part,
+    xs, ps, hs, gs, far, pw, taps, yl, zl, yn, zn,
+    send1, recv1, send2, recv2, plane, column,
     in_sems, out_sems, send_sems, recv_sems,
 ):
     me, mt = lax.axis_index("ctx"), lax.axis_index("tp")
-    n_tp = part.shape[0]
+    n_tp = plane.shape[0] // 2
+    upper, line = me // (CTX // 2), lax.rem(me, CTX // 2)
+    early = line < OWNERS // 2
+    there = lax.rem(mt + n_tp // 2, n_tp)
+    slot = upper * (OWNERS // 2) + line
+    spot = upper * n_tp + mt
     rows, chans = q_in.shape
     cts = chans // LANES
 
@@ -42,13 +49,20 @@
 
     barrier = pltpu.get_barrier_semaphore()
 
-    @pl.loop(1, CTX)
-    def _(off):
-        pl.semaphore_signal(barrier, inc=1, device_id={"ctx": lax.rem(me + off, CTX)}, device_id_type=MESH)
-
-    @pl.loop(1, n_tp)
-    def _(off):
-        pl.semaphore_signal(barrier, inc=1, device_id={"tp": lax.rem(mt + off, n_tp)}, device_id_type=MESH)
+    def in_plane(off):
+        other = lax.rem(spot + off, 2 * n_tp)
+        return {"ctx": other // n_tp * (CTX // 2) + line, "tp": lax.rem(other, n_tp)}
+
+    @pl.when(early)
+    def _():
+        @pl.loop(0, CTX)
+        def _(off):
+            to = {"ctx": lax.rem(me + off, CTX), "tp": there}
+            pl.semaphore_signal(barrier, inc=1, device_id=to, device_id_type=MESH)
+
+        @pl.loop(1, 2 * n_tp)
+        def _(off):
+            pl.semaphore_signal(barrier, inc=1, device_id=in_plane(off), device_id_type=MESH)
 
     def lanes(ct):
         return pl.ds(ct * LANES, LANES)
@@ -68,10 +82,6 @@
     pieces = [(half, ct) for half in range(2) for ct in range(cts)]
     rate = [dec[pl.ds(half * ROWS, ROWS), lanes(ct)] for half, ct in pieces]
     decay = [jnp.exp(-d) for d in rate]
-
-    for (half, ct), d in zip(pieces, rate):
-        for pair in range(4):
-            dt[pl.ds(ct * 64 + 2 * pair + half, ROWS, stride=ROWS), :] = d
 
     def wide(ref, row):
         return jnp.broadcast_to(ref[pl.ds(row, 1), :], (ROWS, LANES))
@@ -99,33 +109,37 @@
     fwd, inner, bwd = lax.fori_loop(0, NSEG, scan_segment, (zeros, zeros, zeros))
 
     for j, (half, ct) in enumerate(pieces):
-        for pair, value in enumerate((fwd[j], bwd[j], inner[j], zeros[j])):
+        for pair, value in enumerate((fwd[j], bwd[j], inner[j], rate[j])):
             send1[pl.ds(ct * 64 + 2 * pair + half, ROWS, stride=ROWS), :] = value
 
     def tile(index):
         return pl.ds(pl.multiple_of(index * ROWS, ROWS), ROWS)
 
-    pl.semaphore_wait(barrier, CTX - 1 + n_tp - 1)
-
-    def exchange(src, dst, which):
-        @pl.loop(1, CTX)
-        def _(off):
-            to = lax.rem(me + off, CTX)
-            pltpu.make_async_remote_copy(
-                src_ref=src.at[tile(to), :],
-                dst_ref=dst.at[tile(me), :],
-                send_sem=send_sems.at[which],
-                recv_sem=recv_sems.at[which],
-                device_id={"ctx": to},
-                device_id_type=MESH,
-            ).start()
-
-    def arrived(dst, sem):
-        most = dst.at[pl.ds(0, (CTX - 1) * ROWS), :]
-        pltpu.make_async_copy(most, most, sem).wait()
-
-    exchange(send1, recv1, 0)
-    recv1[tile(me), :] = send1[tile(me), :]
+    @pl.when(early)
+    def _():
+        pl.semaphore_wait(barrier, OWNERS + 2 * n_tp - 1)
+
+    @pl.when(jnp.logical_not(early))
+    def _():
+        pl.semaphore_wait(barrier, OWNERS)
+
+    def group(index):
+        return pl.ds(pl.multiple_of(index * PIECES * ROWS, PIECES * ROWS), PIECES * ROWS)
+
+    @pl.loop(0, OWNERS)
+    def _(off):
+        to = lax.rem(slot + off, OWNERS)
+        pltpu.make_async_remote_copy(
+            src_ref=send1.at[group(to), :],
+            dst_ref=recv1.at[group(me), :],
+            send_sem=send_sems.at[0],
+            recv_sem=recv_sems.at[0],
+            device_id={"ctx": to // (OWNERS // 2) * (CTX // 2) + lax.rem(to, OWNERS // 2), "tp": there},
+            device_id_type=MESH,
+        ).start()
+
+    def wait_bytes(ref, sem):
+        pltpu.make_async_copy(ref, ref, sem).wait()
 
     unit = [jnp.sqrt(1.0 - jnp.exp(-2.0 * d)) for d in rate]
     coef = [
@@ -166,51 +180,93 @@
                 z = z + p[i + lag] * tap[lag]
             zl[tile(ct * SEG + i), :] = z
 
-    mine = dt[tile(me), :]
-    block = jnp.exp(-float(rows) * mine)
-    step = jnp.exp(-mine)
-    line = lax.broadcasted_iota(jnp.int32, (ROWS, LANES), 0)
-    zero = jnp.zeros((ROWS, LANES), jnp.float32)
-    arrived(recv1, recv_sems.at[0])
-
-    carry, cross, inside = zero, zero, zero
-    for e in range(CTX):
-        got = recv1[pl.ds(e * ROWS, ROWS), :]
-        send2[pl.ds(e * ROWS, ROWS), :] = carry
-        cross = cross + pltpu.roll(got, ROWS - 2, 0) * carry
-        inside = inside + got
-        carry = carry * block + got
-    raw_tile = inside + pltpu.roll(step * cross, 4, 0)
-    carry = zero
-    for e in reversed(range(CTX)):
-        got = recv1[pl.ds(e * ROWS, ROWS), :]
-        before = send2[pl.ds(e * ROWS, ROWS), :]
-        send2[pl.ds(e * ROWS, ROWS), :] = jnp.where(line < 2, before, jnp.where(line < 4, carry, raw_tile))
-        carry = carry * block + got
-
-    exchange(send2, recv2, 1)
-    recv2[tile(me), :] = send2[tile(me), :]
-    arrived(recv2, recv_sems.at[1])
+    row = lax.broadcasted_iota(jnp.int32, (ROWS, LANES), 0)
+
+    @pl.when(early)
+    def _():
+        wait_bytes(recv1, recv_sems.at[0])
+
+        def tiles(ref, e):
+            return [ref[pl.ds((e * PIECES + i) * ROWS, ROWS), :] for i in range(PIECES)]
+
+        def put(e, values):
+            for i, value in enumerate(values):
+                send2[pl.ds((e * PIECES + i) * ROWS, ROWS), :] = value
+
+        rates = [
+            jnp.where(
+                row < 2,
+                pltpu.roll(got, 2, 0),
+                jnp.where(row < 4, pltpu.roll(got, 4, 0), jnp.where(row < 6, pltpu.roll(got, 6, 0), got)),
+            )
+            for got in tiles(recv1, 0)
+        ]
+        block = [jnp.exp(-float(rows) * r) for r in rates]
+        zero = [jnp.zeros((ROWS, LANES), jnp.float32) for _ in rates]
+        carry, cross, inside = list(zero), list(zero), list(zero)
+        for e in range(CTX):
+            put(e, carry)
+            for i, got in enumerate(tiles(recv1, e)):
+                cross[i] = cross[i] + pltpu.roll(got, 6, 0) * carry[i]
+                inside[i] = inside[i] + got
+                carry[i] = carry[i] * block[i] + got
+        raw = [
+            jnp.sqrt(1.0 - jnp.exp(-2.0 * r)) * (inside[i] + pltpu.roll(jnp.exp(-r) * cross[i], 4, 0))
+            for i, r in enumerate(rates)
+        ]
+        carry = list(zero)
+        for e in reversed(range(CTX)):
+            before = tiles(send2, e)
+            put(e, [jnp.where(row < 2, f, jnp.where(row < 4, b, g)) for f, b, g in zip(before, carry, raw)])
+            for i, got in enumerate(tiles(recv1, e)):
+                carry[i] = carry[i] * block[i] + got
+
+        square = jnp.zeros((ROWS, LANES), jnp.float32)
+        for value in raw:
+            square = square + jnp.where((row >= 4) & (row < 6), value * value, 0.0)
+        plane[spot] = jnp.sum(square, axis=0, keepdims=True)
+
+        @pl.loop(1, 2 * n_tp)
+        def _(off):
+            pltpu.make_async_remote_copy(
+                src_ref=plane.at[spot],
+                dst_ref=plane.at[spot],
+                send_sem=send_sems.at[2],
+                recv_sem=recv_sems.at[2],
+                device_id=in_plane(off),
+                device_id_type=MESH,
+            ).start()
+
+        @pl.loop(0, CTX)
+        def _(off):
+            to = lax.rem(me + off, CTX)
+            pltpu.make_async_remote_copy(
+                src_ref=send2.at[group(to), :],
+                dst_ref=recv2.at[group(slot), :],
+                send_sem=send_sems.at[1],
+                recv_sem=recv_sems.at[1],
+                device_id={"ctx": to, "tp": there},
+                device_id_type=MESH,
+            ).start()
+
+        wait_bytes(plane.at[pl.ds(0, 2 * n_tp - 1)], recv_sems.at[2])
+        column[line] = jnp.sum(plane[...], axis=0)
+
+        @pl.loop(1, CTX // 2)
+        def _(off):
+            pltpu.make_async_remote_copy(
+                src_ref=column.at[line],
+                dst_ref=column.at[line],
+                send_sem=send_sems.at[3],
+                recv_sem=recv_sems.at[3],
+                device_id={"ctx": upper * (CTX // 2) + lax.rem(line + off, CTX // 2)},
+                device_id_type=MESH,
+            ).start()
+
+    wait_bytes(recv2, recv_sems.at[1])
 
     def from_owners(pair, half, ct):
         return recv2[pl.ds(ct * 64 + 2 * pair + half, ROWS, stride=ROWS), :]
-
-    raw = [unit[j] * from_owners(2, half, ct) for j, (half, ct) in enumerate(pieces)]
-    square = raw[0] * raw[0]
-    for value in raw[1:]:
-        square = square + value * value
-    part[mt] = jnp.sum(square, axis=0, keepdims=True)
-
-    @pl.loop(1, n_tp)
-    def _(off):
-        pltpu.make_async_remote_copy(
-            src_ref=part.at[mt],
-            dst_ref=part.at[mt],
-            send_sem=send_sems.at[2],
-            recv_sem=recv_sems.at[2],
-            device_id={"tp": lax.rem(mt + off, n_tp)},
-            device_id_type=MESH,
-        ).start()
 
     before = [from_owners(0, half, ct) for half, ct in pieces]
     after = [from_owners(1, half, ct) for half, ct in pieces]
@@ -219,9 +275,9 @@
     def _(r):
         for j, (half, ct) in enumerate(pieces):
             here = pl.ds(pl.multiple_of(ct * rows + r * SEG + half * ROWS, ROWS), ROWS)
-            there = pl.ds(pl.multiple_of(ct * rows + (NSEG - 1 - r) * SEG + half * ROWS, ROWS), ROWS)
+            mirror = pl.ds(pl.multiple_of(ct * rows + (NSEG - 1 - r) * SEG + half * ROWS, ROWS), ROWS)
             hs[here, :] = hs[here, :] + far[here, :] * before[j]
-            gs[here, :] = gs[here, :] + far[there, :] * after[j]
+            gs[here, :] = gs[here, :] + far[mirror, :] * after[j]
 
     def out_copies(at):
         return [
@@ -264,20 +320,43 @@
         for copy in out_copies((slice(None), cols)):
             copy.start()
 
-    others = part.at[pl.ds(0, n_tp - 1)]
-    pltpu.make_async_copy(others, others, recv_sems.at[2]).wait()
-    total = jnp.sum(jnp.sum(part[...], axis=0), axis=1, keepdims=True)
+    half_line = OWNERS // 2
+
+    @pl.when(early)
+    def _():
+        wait_bytes(column.at[pl.ds(0, half_line - 1)], recv_sems.at[3])
+
+    @pl.when(jnp.logical_not(early))
+    def _():
+        wait_bytes(column, recv_sems.at[3])
+
+    total = jnp.sum(jnp.sum(column[...], axis=0), axis=1, keepdims=True)
     factor = jnp.minimum(1.0, math.sqrt(D * ORDER) / jnp.sqrt(total + 1e-06))
     for j, (half, ct) in enumerate(pieces):
-        gr_out[pl.ds(half * ROWS, ROWS), lanes(ct)] = raw[j] * factor
+        gr_out[pl.ds(half * ROWS, ROWS), lanes(ct)] = from_owners(2, half, ct) * factor
     last = pltpu.make_async_copy(gr_out, gr_hbm, out_sems.at[4])
     last.start()
-    arrived(send1, send_sems.at[0])
-    arrived(send2, send_sems.at[1])
-    pltpu.make_async_copy(others, others, send_sems.at[2]).wait()
+    wait_bytes(send1, send_sems.at[0])
+
+    @pl.when(early)
+    def _():
+        wait_bytes(send2, send_sems.at[1])
+        wait_bytes(plane.at[pl.ds(0, 2 * n_tp - 1)], send_sems.at[2])
+        wait_bytes(plane.at[pl.ds(0, CTX // 2 - 1)], send_sems.at[3])
+
     for copy in out_copies((slice(None), slice(None))):
         copy.wait()
     last.wait()
+
+
+def write(*refs):
+    count = len(refs) // 2
+    sems, copies = refs[-1], []
+    for i in range(count):
+        copies.append(pltpu.make_async_copy(refs[i], refs[count + i], sems.at[i]))
+        copies[i].start()
+    for copy in copies:
+        copy.wait()
 
 
 def shards(queries, keys_in, values_in, decay_rates, residues, skip_gain, cotangent):
@@ -292,7 +371,7 @@
     outs = pl.pallas_call(
         kernel,
         out_shape=(line, line, line, line, jax.ShapeDtypeStruct((ORDER, chans), f32)),
-        in_specs=[anywhere] * 7,
+        in_specs=[pl.BlockSpec(memory_space=pltpu.HBM)] * 7,
         out_specs=(anywhere,) * 5,
         scratch_shapes=[
             *[pltpu.VMEM((rows, chans), bf16)] * 4,
@@ -306,16 +385,27 @@
             pltpu.VMEM((cts * (SEG + 1) * ROWS, LANES), f32),
             *[table] * 4,
             posts,
-            *[posts] * 4,
-            pltpu.VMEM((n_tp, 1, LANES), f32),
+            pltpu.VMEM((CTX * PIECES * ROWS, LANES), f32),
+            pltpu.VMEM((CTX * PIECES * ROWS, LANES), f32),
+            posts,
+            pltpu.VMEM((2 * n_tp, 1, LANES), f32),
+            pltpu.VMEM((OWNERS // 2, 1, LANES), f32),
             pltpu.SemaphoreType.DMA((7,)),
             pltpu.SemaphoreType.DMA((5,)),
-            pltpu.SemaphoreType.DMA((3,)),
-            pltpu.SemaphoreType.DMA((3,)),
+            pltpu.SemaphoreType.DMA((4,)),
+            pltpu.SemaphoreType.DMA((4,)),
         ],
-        compiler_params=pltpu.CompilerParams(collective_id=0, has_side_effects=True, vmem_limit_bytes=32 * 2**20),
+        compiler_params=pltpu.CompilerParams(collective_id=0, has_side_effects=True),
         name="modal_conv",
     )(queries, keys_in, values_in, cotangent, decay_rates.T, residues.T, skip_gain.reshape(1, chans))
+    outs = pl.pallas_call(
+        write,
+        out_shape=tuple(jax.ShapeDtypeStruct(o.shape, o.dtype) for o in outs),
+        in_specs=[anywhere] * 5,
+        out_specs=(pl.BlockSpec(memory_space=pltpu.HBM),) * 5,
+        scratch_shapes=[pltpu.SemaphoreType.DMA((5,))],
+        name="write_out",
+    )(*outs)
     return (*outs[:4], outs[4].T)
 
 

time: 48.2 us -> 54.7 us (1.13)
  Pallas kernels: 38.1 us -> 54 us
  local copies, waits for them, and re-layouts: 9.04 us -> 0 us
    pallas_call x0 -> x1, Pallas kernels: none -> 18 us  [shards(): pl.pallas_call(write, out_shape=tuple((jax.ShapeDtypeStruct(o.shape, o.dt...]
    unnamed x19 -> x0, local copies, waits for them, and re-layouts: 9.04 us -> none
    pallas_call x1, Pallas kernels: 38.1 us -> 35.9 us  [shards(): pl.pallas_call(kernel, out_shape=(line, line, line, line, jax.ShapeDtypeS...]
where the time goes in v2:
time: 54.7 us; the launch traced here: 54.6 us
  Pallas kernels  54 us (99%)
  between operations  0.64 us (1%)
    pallas_call x1, Pallas kernels, shards(): pl.pallas_call(kernel, out_shape=(line, line, line, line, jax.ShapeDtypeS...  35.9 us
    pallas_call x1, Pallas kernels, shards(): pl.pallas_call(write, out_shape=tuple((jax.ShapeDtypeStruct(o.shape, o.dt...  18 us

profile of v2, /device:TPU:1, one launch (start us, length us, event | category | flops | bytes accessed | tf_op | source)
XLA Modules:
  0.0 54.6 jit_solution(12879822593193182383)
XLA Ops:
  0.6 35.9 %modal_conv.1 = (bf16[128,512]{1,0:T(8,128)(2,1)}, bf16[128,512]{1,0:T(8,128)(2,1)}, bf16[128,512]{1,0:T(8,128)(2,1)}, bf16[128,512]{1,0:T(8,128)(2,1)}, f32[16,512]{1,0:T(8,128)}) custom-call(bf16[128,512]{1,0:T(8,128)(2,1)} %q_hbm.1, bf16[128,512]{1,0:T(8,128)(2,1)} %k_hbm.1, bf16[128,512]{1,0:T(8,128)(2,1)} %v_hbm.1, bf16[128,512]{1,0:T(8,128)(2,1)} %c_hbm.1, ...), custom_call_target="tpu_custom_call" | custom-call | tf_op jit(solution)/shard_map/modal_conv/pallas_call | solution.py:371
  36.6 18.0 %write_out.1 = (bf16[128,512]{1,0:T(8,128)(2,1)}, bf16[128,512]{1,0:T(8,128)(2,1)}, bf16[128,512]{1,0:T(8,128)(2,1)}, bf16[128,512]{1,0:T(8,128)(2,1)}, f32[16,512]{1,0:T(8,128)}) custom-call(bf16[128,512]{1,0:T(8,128)(2,1)} %get-tuple-element.15.refs_0_, bf16[128,512]{1,0:T(8,128)(2,1)} %get-tuple-element.16.refs_1_, ...), custom_call_target="tpu_custom_call" | custom-call | tf_op jit(solution)/shard_map/write_out/pallas_call | solution.py:401

commit v3 on v2

--- a/solution.py
+++ b/solution.py
@@ -14,8 +14,9 @@
 SEG = 16
 NSEG = 8
 CTX = 32
-OWNERS = 16
-PIECES = 2
+PLANES = 4
+OWNERS = 2 * PLANES
+POST = 32
 MESH = pl.DeviceIdType.MESH
 
 
@@ -25,15 +26,21 @@
     q_in, k_in, v_in, c_in, dec, res, skip,
     op_out, gq_out, gk_out, gv_out, gr_out,
     xs, ps, hs, gs, far, pw, taps, yl, zl, yn, zn,
-    send1, recv1, send2, recv2, plane, column,
+    send1, recv1, send2, recv2, rate_in, plane, column,
     in_sems, out_sems, send_sems, recv_sems,
 ):
     me, mt = lax.axis_index("ctx"), lax.axis_index("tp")
     n_tp = plane.shape[0] // 2
-    upper, line = me // (CTX // 2), lax.rem(me, CTX // 2)
-    early = line < OWNERS // 2
+    half_ctx = CTX // 2
+    upper, line = me // half_ctx, lax.rem(me, half_ctx)
+    floor = line // 2
+
+    def owner_line(up, z):
+        return 2 * z + lax.rem(up + z + 1, 2)
+
+    owner = (floor < PLANES) & (line == owner_line(upper, floor))
     there = lax.rem(mt + n_tp // 2, n_tp)
-    slot = upper * (OWNERS // 2) + line
+    slot = upper * PLANES + floor
     spot = upper * n_tp + mt
     rows, chans = q_in.shape
     cts = chans // LANES
@@ -51,9 +58,10 @@
 
     def in_plane(off):
         other = lax.rem(spot + off, 2 * n_tp)
-        return {"ctx": other // n_tp * (CTX // 2) + line, "tp": lax.rem(other, n_tp)}
-
-    @pl.when(early)
+        up = other // n_tp
+        return {"ctx": up * half_ctx + owner_line(up, floor), "tp": lax.rem(other, n_tp)}
+
+    @pl.when(owner)
     def _():
         @pl.loop(0, CTX)
         def _(off):
@@ -108,33 +116,62 @@
 
     fwd, inner, bwd = lax.fori_loop(0, NSEG, scan_segment, (zeros, zeros, zeros))
 
+    f32, bf16 = jnp.float32, jnp.bfloat16
+
+    def message(first, second, sums):
+        high = sums.astype(bf16)
+        low = (sums - high.astype(f32)).astype(bf16)
+        return jnp.concatenate([first.astype(bf16), second.astype(bf16), high, low], axis=0)
+
+    def parts(ref, index):
+        both = ref[pl.ds(index * POST, POST), :].astype(f32)
+        first, second, high, low = (both[i * ROWS : (i + 1) * ROWS] for i in range(4))
+        return first, second, high + low
+
     for j, (half, ct) in enumerate(pieces):
-        for pair, value in enumerate((fwd[j], bwd[j], inner[j], rate[j])):
-            send1[pl.ds(ct * 64 + 2 * pair + half, ROWS, stride=ROWS), :] = value
+        send1[pl.ds((2 * ct + half) * POST, POST), :] = message(fwd[j], bwd[j], inner[j])
 
     def tile(index):
         return pl.ds(pl.multiple_of(index * ROWS, ROWS), ROWS)
 
-    @pl.when(early)
+    @pl.when(owner)
     def _():
         pl.semaphore_wait(barrier, OWNERS + 2 * n_tp - 1)
 
-    @pl.when(jnp.logical_not(early))
+    @pl.when(jnp.logical_not(owner))
     def _():
         pl.semaphore_wait(barrier, OWNERS)
 
     def group(index):
-        return pl.ds(pl.multiple_of(index * PIECES * ROWS, PIECES * ROWS), PIECES * ROWS)
+        return pl.ds(pl.multiple_of(index * POST, POST), POST)
+
+    rate_at = dec.at[
+        pl.ds(pl.multiple_of(lax.rem(slot, 2) * ROWS, ROWS), ROWS),
+        pl.ds(pl.multiple_of(slot // 2 * LANES, LANES), LANES),
+    ]
+    rate_copy = pltpu.make_async_remote_copy(
+        src_ref=rate_at,
+        dst_ref=rate_in,
+        send_sem=send_sems.at[4],
+        recv_sem=recv_sems.at[4],
+        device_id={"tp": there},
+        device_id_type=MESH,
+    )
+
+    @pl.when(owner)
+    def _():
+        rate_copy.start()
 
     @pl.loop(0, OWNERS)
     def _(off):
         to = lax.rem(slot + off, OWNERS)
+        up, z = to // PLANES, lax.rem(to, PLANES)
         pltpu.make_async_remote_copy(
             src_ref=send1.at[group(to), :],
             dst_ref=recv1.at[group(me), :],
             send_sem=send_sems.at[0],
             recv_sem=recv_sems.at[0],
-            device_id={"ctx": to // (OWNERS // 2) * (CTX // 2) + lax.rem(to, OWNERS // 2), "tp": there},
+            device_id={"ctx": up * half_ctx + owner_line(up, z), "tp": there},
             device_id_type=MESH,
         ).start()
 
@@ -180,51 +217,26 @@
                 z = z + p[i + lag] * tap[lag]
             zl[tile(ct * SEG + i), :] = z
 
-    row = lax.broadcasted_iota(jnp.int32, (ROWS, LANES), 0)
-
-    @pl.when(early)
-    def _():
+    @pl.when(owner)
+    def _():
+        rate_copy.wait_recv()
+        rates = rate_in[...]
+        block = jnp.exp(-float(rows) * rates)
+        step = jnp.exp(-rates)
+        scale = jnp.sqrt(1.0 - jnp.exp(-2.0 * rates))
         wait_bytes(recv1, recv_sems.at[0])
 
-        def tiles(ref, e):
-            return [ref[pl.ds((e * PIECES + i) * ROWS, ROWS), :] for i in range(PIECES)]
-
-        def put(e, values):
-            for i, value in enumerate(values):
-                send2[pl.ds((e * PIECES + i) * ROWS, ROWS), :] = value
-
-        rates = [
-            jnp.where(
-                row < 2,
-                pltpu.roll(got, 2, 0),
-                jnp.where(row < 4, pltpu.roll(got, 4, 0), jnp.where(row < 6, pltpu.roll(got, 6, 0), got)),
-            )
-            for got in tiles(recv1, 0)
-        ]
-        block = [jnp.exp(-float(rows) * r) for r in rates]
-        zero = [jnp.zeros((ROWS, LANES), jnp.float32) for _ in rates]
-        carry, cross, inside = list(zero), list(zero), list(zero)
+        zero = jnp.zeros((ROWS, LANES), f32)
+        ahead = [zero]
+        cross, inside = zero, zero
         for e in range(CTX):
-            put(e, carry)
-            for i, got in enumerate(tiles(recv1, e)):
-                cross[i] = cross[i] + pltpu.roll(got, 6, 0) * carry[i]
-                inside[i] = inside[i] + got
-                carry[i] = carry[i] * block[i] + got
-        raw = [
-            jnp.sqrt(1.0 - jnp.exp(-2.0 * r)) * (inside[i] + pltpu.roll(jnp.exp(-r) * cross[i], 4, 0))
-            for i, r in enumerate(rates)
-        ]
-        carry = list(zero)
-        for e in reversed(range(CTX)):
-            before = tiles(send2, e)
-            put(e, [jnp.where(row < 2, f, jnp.where(row < 4, b, g)) for f, b, g in zip(before, carry, raw)])
-            for i, got in enumerate(tiles(recv1, e)):
-                carry[i] = carry[i] * block[i] + got
-
-        square = jnp.zeros((ROWS, LANES), jnp.float32)
-        for value in raw:
-            square = square + jnp.where((row >= 4) & (row < 6), value * value, 0.0)
-        plane[spot] = jnp.sum(square, axis=0, keepdims=True)
+            start, end, own = parts(recv1, e)
+            cross = cross + end * ahead[e]
+            inside = inside + own
+            ahead.append(ahead[e] * block + start)
+        raw = scale * (inside + step * cross)
+
+        plane[spot] = jnp.sum(raw * raw, axis=0, keepdims=True)
 
         @pl.loop(1, 2 * n_tp)
         def _(off):
@@ -237,9 +249,14 @@
                 device_id_type=MESH,
             ).start()
 
+        carry = zero
+        for e in reversed(range(CTX)):
+            send2[pl.ds(e * POST, POST), :] = message(ahead[e], carry, raw)
+            carry = carry * block + parts(recv1, e)[1]
+
         @pl.loop(0, CTX)
         def _(off):
-            to = lax.rem(me + off, CTX)
+            to = lax.rem(upper + off, 2) * half_ctx + off // 2
             pltpu.make_async_remote_copy(
                 src_ref=send2.at[group(to), :],
                 dst_ref=recv2.at[group(slot), :],
@@ -250,26 +267,25 @@
             ).start()
 
         wait_bytes(plane.at[pl.ds(0, 2 * n_tp - 1)], recv_sems.at[2])
-        column[line] = jnp.sum(plane[...], axis=0)
-
-        @pl.loop(1, CTX // 2)
+        column[floor] = jnp.sum(plane[...], axis=0)
+
+        @pl.loop(1, half_ctx)
         def _(off):
             pltpu.make_async_remote_copy(
-                src_ref=column.at[line],
-                dst_ref=column.at[line],
+                src_ref=column.at[floor],
+                dst_ref=column.at[floor],
                 send_sem=send_sems.at[3],
                 recv_sem=recv_sems.at[3],
-                device_id={"ctx": upper * (CTX // 2) + lax.rem(line + off, CTX // 2)},
+                device_id={"ctx": upper * half_ctx + lax.rem(line + off, half_ctx)},
                 device_id_type=MESH,
             ).start()
 
     wait_bytes(recv2, recv_sems.at[1])
 
-    def from_owners(pair, half, ct):
-        return recv2[pl.ds(ct * 64 + 2 * pair + half, ROWS, stride=ROWS), :]
-
-    before = [from_owners(0, half, ct) for half, ct in pieces]
-    after = [from_owners(1, half, ct) for half, ct in pieces]
+    returned = [parts(recv2, 2 * ct + half) for half, ct in pieces]
+
+    before = [first for first, _, _ in returned]
+    after = [second for _, second, _ in returned]
 
     @pl.loop(0, NSEG)
     def _(r):
@@ -320,26 +336,25 @@
         for copy in out_copies((slice(None), cols)):
             copy.start()
 
-    half_line = OWNERS // 2
-
-    @pl.when(early)
-    def _():
-        wait_bytes(column.at[pl.ds(0, half_line - 1)], recv_sems.at[3])
-
-    @pl.when(jnp.logical_not(early))
+    @pl.when(owner)
+    def _():
+        wait_bytes(column.at[pl.ds(0, PLANES - 1)], recv_sems.at[3])
+
+    @pl.when(jnp.logical_not(owner))
     def _():
         wait_bytes(column, recv_sems.at[3])
 
     total = jnp.sum(jnp.sum(column[...], axis=0), axis=1, keepdims=True)
     factor = jnp.minimum(1.0, math.sqrt(D * ORDER) / jnp.sqrt(total + 1e-06))
     for j, (half, ct) in enumerate(pieces):
-        gr_out[pl.ds(half * ROWS, ROWS), lanes(ct)] = from_owners(2, half, ct) * factor
+        gr_out[pl.ds(half * ROWS, ROWS), lanes(ct)] = parts(recv2, 2 * ct + half)[2] * factor
     last = pltpu.make_async_copy(gr_out, gr_hbm, out_sems.at[4])
     last.start()
     wait_bytes(send1, send_sems.at[0])
 
-    @pl.when(early)
-    def _():
+    @pl.when(owner)
+    def _():
+        rate_copy.wait_send()
         wait_bytes(send2, send_sems.at[1])
         wait_bytes(plane.at[pl.ds(0, 2 * n_tp - 1)], send_sems.at[2])
         wait_bytes(plane.at[pl.ds(0, CTX // 2 - 1)], send_sems.at[3])
@@ -364,13 +379,12 @@
     n_tp = lax.axis_size("tp")
     cts = chans // LANES
     f32, bf16 = jnp.float32, jnp.bfloat16
-    line = jax.ShapeDtypeStruct((rows, chans), bf16)
+    line = pltpu.VMEM((rows, chans), bf16)
     anywhere = pl.BlockSpec(memory_space=pl.ANY)
     table = pltpu.VMEM((cts * rows, LANES), f32)
-    posts = pltpu.VMEM((CTX * ROWS, LANES), f32)
     outs = pl.pallas_call(
         kernel,
-        out_shape=(line, line, line, line, jax.ShapeDtypeStruct((ORDER, chans), f32)),
+        out_shape=(line, line, line, line, pltpu.VMEM((ORDER, chans), f32)),
         in_specs=[pl.BlockSpec(memory_space=pltpu.HBM)] * 7,
         out_specs=(anywhere,) * 5,
         scratch_shapes=[
@@ -384,20 +398,26 @@
             pltpu.VMEM((cts * (SEG + 1) * ORDER, LANES), f32),
             pltpu.VMEM((cts * (SEG + 1) * ROWS, LANES), f32),
             *[table] * 4,
-            posts,
-            pltpu.VMEM((CTX * PIECES * ROWS, LANES), f32),
-            pltpu.VMEM((CTX * PIECES * ROWS, LANES), f32),
-            posts,
+            pltpu.VMEM((OWNERS * POST, LANES), bf16),
+            pltpu.VMEM((CTX * POST, LANES), bf16),
+            pltpu.VMEM((CTX * POST, LANES), bf16),
+            pltpu.VMEM((OWNERS * POST, LANES), bf16),
+            pltpu.VMEM((ROWS, LANES), f32),
             pltpu.VMEM((2 * n_tp, 1, LANES), f32),
-            pltpu.VMEM((OWNERS // 2, 1, LANES), f32),
+            pltpu.VMEM((PLANES, 1, LANES), f32),
             pltpu.SemaphoreType.DMA((7,)),
             pltpu.SemaphoreType.DMA((5,)),
-            pltpu.SemaphoreType.DMA((4,)),
-            pltpu.SemaphoreType.DMA((4,)),
+            pltpu.SemaphoreType.DMA((5,)),
+            pltpu.SemaphoreType.DMA((5,)),
         ],
-        compiler_params=pltpu.CompilerParams(collective_id=0, has_side_effects=True),
+        compiler_params=pltpu.CompilerParams(collective_id=0, has_side_effects=True, vmem_limit_bytes=16 * 2**20),
         name="modal_conv",
-    )(queries, keys_in, values_in, cotangent, decay_rates.T, residues.T, skip_gain.reshape(1, chans))
+    )(
+        *[
+            pltpu.with_memory_space_constraint(x, pltpu.HBM)
+            for x in (queries, keys_in, values_in, cotangent, decay_rates.T, residues.T, skip_gain.reshape(1, chans))
+        ]
+    )
     outs = pl.pallas_call(
         write,
         out_shape=tuple(jax.ShapeDtypeStruct(o.shape, o.dtype) for o in outs),
@@ -405,7 +425,8 @@
         out_specs=(pl.BlockSpec(memory_space=pltpu.HBM),) * 5,
         scratch_shapes=[pltpu.SemaphoreType.DMA((5,))],
         name="write_out",
-    )(*outs)
+        compiler_params=pltpu.CompilerParams(vmem_limit_bytes=4 * 2**20),
+    )(*[pltpu.with_memory_space_constraint(x, pltpu.VMEM) for x in outs])
     return (*outs[:4], outs[4].T)
 
 

time: 54.7 us -> 32 us (0.59)
  Pallas kernels: 54 us -> 31.2 us
    pallas_call x1, Pallas kernels: 18 us -> 0.83 us  [shards(): pl.pallas_call(write, out_shape=tuple((jax.ShapeDtypeStruct(o.shape, o.dt...]
    pallas_call x1, Pallas kernels: 35.9 us -> 30.4 us  [shards(): pl.pallas_call(kernel, out_shape=(line, line, line, line, pltpu.VMEM((ORD...]
where the time goes in v3:
time: 32 us; the launch traced here: 31.9 us
  Pallas kernels  31.2 us (98%)
  between operations  0.64 us (2%)
    pallas_call x1, Pallas kernels, shards(): pl.pallas_call(kernel, out_shape=(line, line, line, line, pltpu.VMEM((ORD...  30.4 us
    pallas_call x1, Pallas kernels, shards(): pl.pallas_call(write, out_shape=tuple((jax.ShapeDtypeStruct(o.shape, o.dt...  0.83 us

profile of v3, /device:TPU:1, one launch (start us, length us, event | category | flops | bytes accessed | tf_op | source)
XLA Modules:
  0.0 31.9 jit_solution(6891517524313069170)
XLA Ops:
  0.6 30.4 %modal_conv.1 = (bf16[128,512]{1,0:T(8,128)(2,1)S(1)}, bf16[128,512]{1,0:T(8,128)(2,1)S(1)}, bf16[128,512]{1,0:T(8,128)(2,1)S(1)}, bf16[128,512]{1,0:T(8,128)(2,1)S(1)}, f32[16,512]{1,0:T(8,128)S(1)}) custom-call(bf16[128,512]{1,0:T(8,128)(2,1)} %q_hbm.1, bf16[128,512]{1,0:T(8,128)(2,1)} %k_hbm.1, bf16[128,512]{1,0:T(8,128)(2,1)} %v_hbm.1, ...), custom_call_target="tpu_custom_call" | custom-call | tf_op jit(solution)/shard_map/modal_conv/pallas_call | solution.py:385
  31.0 0.8 %write_out.1 = (bf16[128,512]{1,0:T(8,128)(2,1)}, bf16[128,512]{1,0:T(8,128)(2,1)}, bf16[128,512]{1,0:T(8,128)(2,1)}, bf16[128,512]{1,0:T(8,128)(2,1)}, f32[16,512]{1,0:T(8,128)}) custom-call(bf16[128,512]{1,0:T(8,128)(2,1)S(1)} %get-tuple-element.15.refs_0_, bf16[128,512]{1,0:T(8,128)(2,1)S(1)} %get-tuple-element.16.refs_1_, ...), custom_call_target="tpu_custom_call" | custom-call | tf_op jit(solution)/shard_map/write_out/pallas_call | solution.py:421

commit v4 on v3

v4 whole, which is shorter than its diff:
```python
import math

import jax
import jax.numpy as jnp
from jax import lax
from jax.experimental import pallas as pl
from jax.experimental.pallas import tpu as pltpu
from jax.sharding import PartitionSpec as P

D = 8192
ORDER = 16
LANES = 128
ROWS = 8
SEG = 16
NSEG = 8
CHUNKS = 4
CTX = 32
PLANES = 2
OWNERS = 2 * PLANES
POST = 3 * ORDER
BACK = 2 * ORDER
MESH = pl.DeviceIdType.MESH


def kernel(
    q_hbm, k_hbm, v_hbm, c_hbm, dec_hbm, res_hbm, skip_hbm,
    op_out, gq_out, gk_out, gv_out, gr_out,
    q_in, k_in, v_in, c_in, dec, res, skip,
    xs, ps, hs, gs, far, raf, carries, pw, taps, yl, zl, yn, zn,
    send1, recv1, send2, recv2, send3, recv3, rate_in, plane, column,
    in_sems, send_sems, recv_sems,
):
    me, mt = lax.axis_index("ctx"), lax.axis_index("tp")
    n_tp = plane.shape[0] // (2 * PLANES)
    chips = 2 * n_tp
    half_ctx = CTX // 2
    upper, line = me // half_ctx, lax.rem(me, half_ctx)
    floor = line // 2
    owner = (floor < PLANES) & (lax.rem(line, 2) == 0)
    there = lax.rem(mt + n_tp // 2, n_tp)
    slot = upper * PLANES + floor
    spot = upper * n_tp + mt
    rows, chans = q_in.shape
    cts = chans // LANES

    def fetch(src, dst, sem):
        return pltpu.make_async_copy(src, dst, sem)

    fetch(dec_hbm, dec, in_sems.at[CHUNKS]).start()
    chunk = rows // CHUNKS
    for i in range(CHUNKS):
        at = pl.ds(i * chunk, chunk)
        for src, dst in ((k_hbm, k_in), (v_hbm, v_in), (q_hbm, q_in), (c_hbm, c_in)):
            fetch(src.at[at, :], dst.at[at, :], in_sems.at[i]).start()
    fetch(res_hbm, res, in_sems.at[CHUNKS + 1]).start()
    fetch(skip_hbm, skip, in_sems.at[CHUNKS + 2]).start()

    barrier = pltpu.get_barrier_semaphore()

    ground = floor == 0

    def in_plane(index, cores, z):
        chip, core = index // cores, lax.rem(index, cores)
        return {"ctx": chip // n_tp * half_ctx + 2 * z + core, "tp": lax.rem(chip, n_tp)}

    def signal(to):
        pl.semaphore_signal(barrier, inc=1, device_id=to, device_id_type=MESH)

    @pl.when(owner)
    def _():
        @pl.loop(0, CTX)
        def _(off):
            signal({"ctx": lax.rem(me + off, CTX), "tp": there})

    is_target = ground & owner

    @pl.when(ground)
    def _():
        @pl.loop(1, chips)
        def _(off):
            signal(in_plane(lax.rem(spot + off, chips), 1, 0))

        @pl.loop(0, chips)
        def _(off):
            signal(in_plane(lax.rem(spot + off, chips), 1, 1))

        @pl.when(jnp.logical_not(owner))
        def _():
            signal(in_plane(spot, 1, 0))

    def lanes(ct):
        return pl.ds(ct * LANES, LANES)

    fetch(dec_hbm, dec, in_sems.at[CHUNKS]).wait()

    pieces = [(half, ct) for half in range(2) for ct in range(cts)]
    rate = [dec[pl.ds(half * ROWS, ROWS), lanes(ct)] for half, ct in pieces]
    decay = [jnp.exp(-d) for d in rate]

    def wide(ref, row):
        return jnp.broadcast_to(ref[pl.ds(row, 1), :], (ROWS, LANES))

    zeros = [jnp.zeros((ROWS, LANES), jnp.float32) for _ in pieces]

    block16 = [jnp.exp(-float(SEG) * d) for d in rate]

    def scan_chunk(i, state):
        fwd, inner, back, far_off = (list(part_) for part_ in state)
        fetch(k_in, k_in, in_sems.at[i]).wait()
        first = i * chunk
        for sub in range(chunk // SEG):
            for ct in range(cts):
                at = (pl.ds(pl.multiple_of(first + sub * SEG, SEG), SEG), lanes(ct))
                to = pl.ds(pl.multiple_of(ct * rows + first + sub * SEG, SEG), SEG)
                kv = k_in[at].astype(jnp.float32) * v_in[at].astype(jnp.float32)
                cq = c_in[at].astype(jnp.float32) * q_in[at].astype(jnp.float32)
                xs[to, :] = kv.astype(jnp.bfloat16).astype(jnp.float32)
                ps[to, :] = cq.astype(jnp.bfloat16).astype(jnp.float32)
        for sub in range(chunk // SEG):
            start = first + sub * SEG
            for j, (half, ct) in enumerate(pieces):
                hs[pl.ds(pl.multiple_of(ct * rows + start + half * ROWS, ROWS), ROWS), :] = fwd[j]
            own = list(zeros)
            for i2 in range(SEG):
                for ct in range(cts):
                    x = wide(xs, ct * rows + start + i2)
                    p = wide(ps, ct * rows + start + i2)
                    pb = wide(ps, ct * rows + start + (SEG - 1 - i2))
                    for half in range(2):
                        j = half * cts + ct
                        fwd[j] = fwd[j] * decay[j] + x
                        inner[j] = inner[j] + fwd[j] * p
                        own[j] = own[j] * decay[j] + pb
            for j, (half, ct) in enumerate(pieces):
                gs[pl.ds(pl.multiple_of(ct * rows + start + half * ROWS, ROWS), ROWS), :] = own[j]
                back[j] = back[j] + far_off[j] * own[j]
                far_off[j] = far_off[j] * block16[j]
        return fwd, inner, back, far_off

    ones = [jnp.ones((ROWS, LANES), jnp.float32) for _ in pieces]
    fwd, inner, bwd, _ = lax.fori_loop(0, CHUNKS, scan_chunk, (zeros, zeros, zeros, ones))

    f32, bf16 = jnp.float32, jnp.bfloat16

    for j, (half, ct) in enumerate(pieces):
        if half == 0:
            for i, states in enumerate((fwd, bwd, inner)):
                both = jnp.concatenate([states[j], states[j + cts]], axis=0)
                send1[pl.ds(ct * POST + i * ORDER, ORDER), :] = both.astype(bf16)

    def tile(index):
        return pl.ds(pl.multiple_of(index * ROWS, ROWS), ROWS)

    @pl.when(is_target)
    def _():
        pl.semaphore_wait(barrier, OWNERS + 2 * chips - 1)

    @pl.when(owner & jnp.logical_not(ground))
    def _():
        pl.semaphore_wait(barrier, OWNERS + 2 * chips)

    @pl.when(jnp.logical_not(owner))
    def _():
        pl.semaphore_wait(barrier, OWNERS)

    def group(index, size):
        return pl.ds(pl.multiple_of(index * size, size), size)

    rate_at = dec.at[:, pl.ds(pl.multiple_of(slot * LANES, LANES), LANES)]
    rate_copy = pltpu.make_async_remote_copy(
        src_ref=rate_at,
        dst_ref=rate_in,
        send_sem=send_sems.at[4],
        recv_sem=recv_sems.at[4],
        device_id={"tp": there},
        device_id_type=MESH,
    )

    @pl.when(owner)
    def _():
        rate_copy.start()

    @pl.loop(0, OWNERS)
    def _(off):
        to = lax.rem(slot + off, OWNERS)
        pltpu.make_async_remote_copy(
            src_ref=send1.at[group(to, POST), :],
            dst_ref=recv1.at[group(me, POST), :],
            send_sem=send_sems.at[0],
            recv_sem=recv_sems.at[0],
            device_id={"ctx": to // PLANES * half_ctx + 2 * lax.rem(to, PLANES), "tp": there},
            device_id_type=MESH,
        ).start()

    def wait_bytes(ref, sem):
        pltpu.make_async_copy(ref, ref, sem).wait()

    fetch(res_hbm, res, in_sems.at[CHUNKS + 1]).wait()
    fetch(skip_hbm, skip, in_sems.at[CHUNKS + 2]).wait()

    def chain_back(i, after):
        r = NSEG - 1 - i
        new = []
        for j, (half, ct) in enumerate(pieces):
            here = pl.ds(pl.multiple_of(ct * rows + r * SEG + half * ROWS, ROWS), ROWS)
            own = gs[here, :]
            gs[here, :] = after[j]
            new.append(after[j] * block16[j] + own)
        return new

    lax.fori_loop(0, NSEG, chain_back, zeros)
    unit = [jnp.sqrt(1.0 - jnp.exp(-2.0 * d)) for d in rate]
    coef = [
        res[pl.ds(half * ROWS, ROWS), lanes(ct)] * unit[j] for j, (half, ct) in enumerate(pieces)
    ]

    @pl.loop(0, SEG + 1)
    def _(i):
        lag = i.astype(jnp.float32)
        for ct in range(cts):
            total = None
            for half in range(2):
                j = half * cts + ct
                power = coef[j] * jnp.exp(-rate[j] * lag)
                pw[pl.ds(pl.multiple_of((ct * (SEG + 1) + i) * ORDER + half * ROWS, ROWS), ROWS), :] = power
                total = power if total is None else total + power
            total = jnp.sum(total, axis=0, keepdims=True)
            taps[tile(ct * (SEG + 1) + i), :] = jnp.broadcast_to(total, (ROWS, LANES))

    @pl.loop(0, NSEG)
    def _(r):
        lag = (r * SEG).astype(jnp.float32)
        for j, (half, ct) in enumerate(pieces):
            power = jnp.exp(-rate[j] * lag)
            far[pl.ds(pl.multiple_of(ct * rows + r * SEG + half * ROWS, ROWS), ROWS), :] = power
            mirror = ct * rows + (NSEG - 1 - r) * SEG + half * ROWS
            raf[pl.ds(pl.multiple_of(mirror, ROWS), ROWS), :] = power

    @pl.loop(0, cts)
    def _(ct):
        x = [xs[pl.ds(ct * rows + i, NSEG, stride=SEG), :] for i in range(SEG)]
        p = [ps[pl.ds(ct * rows + i, NSEG, stride=SEG), :] for i in range(SEG)]
        tap = [taps[tile(ct * (SEG + 1) + i), :] for i in range(SEG)]
        for i in range(SEG):
            y = x[i] * tap[0]
            for lag in range(1, i + 1):
                y = y + x[i - lag] * tap[lag]
            yl[tile(ct * SEG + i), :] = y
            z = p[i] * tap[0]
            for lag in range(1, SEG - i):
                z = z + p[i + lag] * tap[lag]
            zl[tile(ct * SEG + i), :] = z

    @pl.when(owner)
    def _():
        rate_copy.wait_recv()
        rates = rate_in[...]
        block = jnp.exp(-float(rows) * rates)
        step = jnp.exp(-rates)
        scale = jnp.sqrt(1.0 - jnp.exp(-2.0 * rates))
        wait_bytes(recv1, recv_sems.at[0])

        def came(e, i):
            return recv1[pl.ds(e * POST + i * ORDER, ORDER), :].astype(f32)

        zero = jnp.zeros((ORDER, LANES), f32)
        carry, back, cross, inside = zero, zero, zero, zero
        for e in range(CTX):
            last = CTX - 1 - e
            send2[pl.ds(e * BACK, ORDER), :] = carry.astype(bf16)
            send2[pl.ds(last * BACK + ORDER, ORDER), :] = back.astype(bf16)
            cross = cross + came(e, 1) * carry
            inside = inside + came(e, 2)
            carry = carry * block + came(e, 0)
            back = back * block + came(last, 1)
        raw = scale * (inside + step * cross)
        send3[...] = raw

        part = floor * chips + spot
        plane[part] = jnp.sum(raw * raw, axis=0, keepdims=True)

        def tell(to):
            pltpu.make_async_remote_copy(
                src_ref=plane.at[part],
                dst_ref=plane.at[part],
                send_sem=send_sems.at[2],
                recv_sem=recv_sems.at[2],
                device_id=to,
                device_id_type=MESH,
            ).start()

        @pl.loop(2, 2 * chips)
        def _(off):
            tell(in_plane(lax.rem(2 * spot + off, 2 * chips), 2, 0))

        tell(in_plane(2 * spot + 1, 2, 0))

        @pl.when(jnp.logical_not(ground))
        def _():
            tell(in_plane(2 * spot, 2, 0))

        @pl.loop(0, CTX)
        def _(off):
            to = lax.rem(upper + off, 2) * half_ctx + off // 2
            for src, dst, which in (
                (send2.at[group(to, BACK), :], recv2.at[group(slot, BACK), :], 1),
                (send3, recv3.at[group(slot, ORDER), :], 5),
            ):
                pltpu.make_async_remote_copy(
                    src_ref=src,
                    dst_ref=dst,
                    send_sem=send_sems.at[which],
                    recv_sem=recv_sems.at[which],
                    device_id={"ctx": to, "tp": there},
                    device_id_type=MESH,
                ).start()

    wait_bytes(recv2, recv_sems.at[1])

    carries[...] = recv2[...].astype(f32)

    @pl.loop(0, cts)
    def _(ct):
        def edges(near, power, n, which):
            at = pl.ds(ct * rows + n, NSEG, stride=SEG)
            return near[at, :] + power[at, :] * wide(carries, ct * BACK + which * ORDER + n)

        h = [edges(hs, far, n, 0) for n in range(ORDER)]
        g = [edges(gs, raf, n, 1) for n in range(ORDER)]
        for i in range(SEG):
            y = yl[tile(ct * SEG + i), :]
            z = zl[tile(ct * SEG + SEG - 1 - i), :]
            ys, zs = [], []
            for n in range(ORDER):
                power = wide(pw, (ct * (SEG + 1) + i + 1) * ORDER + n)
                ys.append(power * h[n])
                zs.append(power * g[n])
            while len(ys) > 1:
                ys = [a + b for a, b in zip(ys[::2], ys[1::2])]
                zs = [a + b for a, b in zip(zs[::2], zs[1::2])]
            yn[pl.ds(ct * rows + i, NSEG, stride=SEG), :] = y + ys[0]
            zn[pl.ds(ct * rows + SEG - 1 - i, NSEG, stride=SEG), :] = z + zs[0]
        cols = pl.ds(pl.multiple_of(ct * LANES, LANES), LANES)
        gain = jnp.broadcast_to(skip[:, cols], (SEG, LANES))
        for r in range(rows // SEG):
            at = (pl.ds(r * SEG, SEG), cols)
            here = pl.ds(pl.multiple_of(ct * rows + r * SEG, SEG), SEG)
            conv = yn[here, :].astype(jnp.bfloat16).astype(jnp.float32)
            adj = zn[here, :].astype(jnp.bfloat16).astype(jnp.float32)
            mixed = conv + gain * xs[here, :]
            grad = adj + gain * ps[here, :]
            op_out[at] = (q_in[at].astype(jnp.float32) * mixed).astype(jnp.bfloat16)
            gq_out[at] = (c_in[at].astype(jnp.float32) * mixed).astype(jnp.bfloat16)
            gk_out[at] = (v_in[at].astype(jnp.float32) * grad).astype(jnp.bfloat16)
            gv_out[at] = (k_in[at].astype(jnp.float32) * grad).astype(jnp.bfloat16)

    @pl.when(ground)
    def _():
        @pl.when(owner)
        def _():
            wait_bytes(plane.at[pl.ds(0, 2 * chips - 1)], recv_sems.at[2])

        @pl.when(jnp.logical_not(owner))
        def _():
            wait_bytes(plane, recv_sems.at[2])

        column[...] = jnp.sum(plane[...], axis=0)

        @pl.when(owner)
        def _():
            @pl.loop(2, half_ctx)
            def _(off):
                pltpu.make_async_remote_copy(
                    src_ref=column,
                    dst_ref=column,
                    send_sem=send_sems.at[3],
                    recv_sem=recv_sems.at[3],
                    device_id={"ctx": upper * half_ctx + off},
                    device_id_type=MESH,
                ).start()

    @pl.when(jnp.logical_not(ground))
    def _():
        wait_bytes(column, recv_sems.at[3])

    wait_bytes(recv3, recv_sems.at[5])
    total = jnp.sum(column[...], axis=1, keepdims=True)
    factor = jnp.minimum(1.0, math.sqrt(D * ORDER) / jnp.sqrt(total + 1e-06))
    for ct in range(cts):
        gr_out[:, lanes(ct)] = recv3[pl.ds(ct * ORDER, ORDER), :] * factor
    wait_bytes(send1, send_sems.at[0])

    @pl.when(owner)
    def _():
        rate_copy.wait_send()
        wait_bytes(send2, send_sems.at[1])
        wait_bytes(xs.at[pl.ds(0, CTX * ORDER), :], send_sems.at[5])

    @pl.when(is_target)
    def _():
        wait_bytes(plane.at[pl.ds(0, 2 * chips - 1)], send_sems.at[2])
        wait_bytes(plane.at[pl.ds(0, half_ctx - 2)], send_sems.at[3])

    @pl.when(owner & jnp.logical_not(ground))
    def _():
        wait_bytes(plane, send_sems.at[2])


def write(*refs):
    count = len(refs) // 2
    sems, copies = refs[-1], []
    for i in range(count):
        copies.append(pltpu.make_async_copy(refs[i], refs[count + i], sems.at[i]))
        copies[i].start()
    for copy in copies:
        copy.wait()


def shards(queries, keys_in, values_in, decay_rates, residues, skip_gain, cotangent):
    rows, chans = queries.shape
    n_tp = lax.axis_size("tp")
    cts = chans // LANES
    f32, bf16 = jnp.float32, jnp.bfloat16
    line = pltpu.VMEM((rows, chans), bf16)
    anywhere = pl.BlockSpec(memory_space=pl.ANY)
    table = pltpu.VMEM((cts * rows, LANES), f32)
    outs = pl.pallas_call(
        kernel,
        out_shape=(line, line, line, line, pltpu.VMEM((ORDER, chans), f32)),
        in_specs=[pl.BlockSpec(memory_space=pltpu.HBM)] * 7,
        out_specs=(pl.BlockSpec(memory_space=pltpu.VMEM),) * 5,
        scratch_shapes=[
            *[pltpu.VMEM((rows, chans), bf16)] * 4,
            pltpu.VMEM((ORDER, chans), f32),
            pltpu.VMEM((ORDER, chans), f32),
            pltpu.VMEM((1, chans), f32),
            *[table] * 6,
            pltpu.VMEM((OWNERS * BACK, LANES), f32),
            pltpu.VMEM((cts * (SEG + 1) * ORDER, LANES), f32),
            pltpu.VMEM((cts * (SEG + 1) * ROWS, LANES), f32),
            *[table] * 4,
            pltpu.VMEM((OWNERS * POST, LANES), bf16),
            pltpu.VMEM((CTX * POST, LANES), bf16),
            pltpu.VMEM((CTX * BACK, LANES), bf16),
            pltpu.VMEM((OWNERS * BACK, LANES), bf16),
            pltpu.VMEM((ORDER, LANES), f32),
            pltpu.VMEM((OWNERS * ORDER, LANES), f32),
            pltpu.VMEM((ORDER, LANES), f32),
            pltpu.VMEM((2 * n_tp * PLANES, 1, LANES), f32),
            pltpu.VMEM((1, LANES), f32),
            pltpu.SemaphoreType.DMA((CHUNKS + 3,)),
            pltpu.SemaphoreType.DMA((6,)),
            pltpu.SemaphoreType.DMA((6,)),
        ],
        compiler_params=pltpu.CompilerParams(collective_id=0, has_side_effects=True, vmem_limit_bytes=16 * 2**20),
        name="modal_conv",
    )(
        *[
            pltpu.with_memory_space_constraint(x, pltpu.HBM)
            for x in (queries, keys_in, values_in, cotangent, decay_rates.T, residues.T, skip_gain.reshape(1, chans))
        ]
    )
    outs = pl.pallas_call(
        write,
        out_shape=tuple(jax.ShapeDtypeStruct(o.shape, o.dtype) for o in outs),
        in_specs=[anywhere] * 5,
        out_specs=(pl.BlockSpec(memory_space=pltpu.HBM),) * 5,
        scratch_shapes=[pltpu.SemaphoreType.DMA((5,))],
        name="write_out",
        compiler_params=pltpu.CompilerParams(vmem_limit_bytes=4 * 2**20),
    )(*[pltpu.with_memory_space_constraint(x, pltpu.VMEM) for x in outs])
    return (*outs[:4], outs[4].T)


def solution(mesh):
    line, modes = P("ctx", "tp"), P("tp", None)
    in_specs = (line, line, line, modes, modes, P("tp"), line)
    out_specs = (line, line, line, line, modes)
    return jax.shard_map(shards, mesh=mesh, in_specs=in_specs, out_specs=out_specs, check_vma=False)
```

time: 32 us -> 30.1 us (0.941); the launches traced: 31.9 us -> 29.6 us
  Pallas kernels: 31.2 us -> 29 us
    pallas_call x1, Pallas kernels: 30.4 us -> 28.1 us  [shards(): pl.pallas_call(kernel, out_shape=(line, line, line, line, pltpu.VMEM((ORD...]
where the time goes in v4:
time: 30.1 us; the launch traced here: 29.6 us
  Pallas kernels  29 us (96%)
  between operations  0.64 us (2%)
    pallas_call x1, Pallas kernels, shards(): pl.pallas_call(kernel, out_shape=(line, line, line, line, pltpu.VMEM((ORD...  28.1 us
    pallas_call x1, Pallas kernels, shards(): pl.pallas_call(write, out_shape=tuple((jax.ShapeDtypeStruct(o.shape, o.dt...  0.83 us

profile of v4, /device:TPU:1, one launch (start us, length us, event | category | flops | bytes accessed | tf_op | source)
XLA Modules:
  0.0 29.6 jit_solution(14398643407974030520)
XLA Ops:
  0.6 28.1 %modal_conv.1 = (bf16[128,512]{1,0:T(8,128)(2,1)S(1)}, bf16[128,512]{1,0:T(8,128)(2,1)S(1)}, bf16[128,512]{1,0:T(8,128)(2,1)S(1)}, bf16[128,512]{1,0:T(8,128)(2,1)S(1)}, f32[16,512]{1,0:T(8,128)S(1)}) custom-call(bf16[128,512]{1,0:T(8,128)(2,1)} %q_hbm.1, bf16[128,512]{1,0:T(8,128)(2,1)} %k_hbm.1, bf16[128,512]{1,0:T(8,128)(2,1)} %v_hbm.1, ...), custom_call_target="tpu_custom_call" | custom-call | tf_op jit(solution)/shard_map/modal_conv/pallas_call | solution.py:427
  28.8 0.8 %write_out.1 = (bf16[128,512]{1,0:T(8,128)(2,1)}, bf16[128,512]{1,0:T(8,128)(2,1)}, bf16[128,512]{1,0:T(8,128)(2,1)}, bf16[128,512]{1,0:T(8,128)(2,1)}, f32[16,512]{1,0:T(8,128)}) custom-call(bf16[128,512]{1,0:T(8,128)(2,1)S(1)} %get-tuple-element.15.refs_0_, bf16[128,512]{1,0:T(8,128)(2,1)S(1)} %get-tuple-element.16.refs_1_, ...), custom_call_target="tpu_custom_call" | custom-call | tf_op jit(solution)/shard_map/write_out/pallas_call | solution.py:463

commit v5 on v4

--- a/solution.py
+++ b/solution.py
@@ -59,34 +59,37 @@
 
     ground = floor == 0
 
-    def in_plane(index, cores, z):
-        chip, core = index // cores, lax.rem(index, cores)
-        return {"ctx": chip // n_tp * half_ctx + 2 * z + core, "tp": lax.rem(chip, n_tp)}
-
-    def signal(to):
-        pl.semaphore_signal(barrier, inc=1, device_id=to, device_id_type=MESH)
+    here, over = upper * half_ctx, (1 - upper) * half_ctx
+
+    def signal(ctx, tp):
+        pl.semaphore_signal(barrier, inc=1, device_id={"ctx": ctx, "tp": tp}, device_id_type=MESH)
 
     @pl.when(owner)
     def _():
-        @pl.loop(0, CTX)
+        @pl.loop(0, half_ctx)
         def _(off):
-            signal({"ctx": lax.rem(me + off, CTX), "tp": there})
+            signal(over + off, there)
+            signal(here + off, there)
 
     is_target = ground & owner
 
     @pl.when(ground)
     def _():
-        @pl.loop(1, chips)
+        @pl.loop(1, n_tp)
         def _(off):
-            signal(in_plane(lax.rem(spot + off, chips), 1, 0))
-
-        @pl.loop(0, chips)
-        def _(off):
-            signal(in_plane(lax.rem(spot + off, chips), 1, 1))
+            tp = lax.rem(mt + off, n_tp)
+            for z in range(PLANES):
+                signal(over + 2 * z, tp)
+                signal(here + 2 * z, tp)
+
+        signal(over, mt)
+        for z in range(1, PLANES):
+            signal(over + 2 * z, mt)
+            signal(here + 2 * z, mt)
 
         @pl.when(jnp.logical_not(owner))
         def _():
-            signal(in_plane(spot, 1, 0))
+            signal(here, mt)
 
     def lanes(ct):
         return pl.ds(ct * LANES, LANES)
@@ -180,17 +183,17 @@
     def _():
         rate_copy.start()
 
-    @pl.loop(0, OWNERS)
-    def _(off):
-        to = lax.rem(slot + off, OWNERS)
-        pltpu.make_async_remote_copy(
-            src_ref=send1.at[group(to, POST), :],
-            dst_ref=recv1.at[group(me, POST), :],
-            send_sem=send_sems.at[0],
-            recv_sem=recv_sems.at[0],
-            device_id={"ctx": to // PLANES * half_ctx + 2 * lax.rem(to, PLANES), "tp": there},
-            device_id_type=MESH,
-        ).start()
+    for half_at in (over, here):
+        for z in reversed(range(PLANES)):
+            to = half_at // half_ctx * PLANES + z
+            pltpu.make_async_remote_copy(
+                src_ref=send1.at[group(to, POST), :],
+                dst_ref=recv1.at[group(me, POST), :],
+                send_sem=send_sems.at[0],
+                recv_sem=recv_sems.at[0],
+                device_id={"ctx": half_at + 2 * z, "tp": there},
+                device_id_type=MESH,
+            ).start()
 
     def wait_bytes(ref, sem):
         pltpu.make_async_copy(ref, ref, sem).wait()
@@ -279,41 +282,47 @@
         part = floor * chips + spot
         plane[part] = jnp.sum(raw * raw, axis=0, keepdims=True)
 
-        def tell(to):
+        def tell(ctx, tp):
             pltpu.make_async_remote_copy(
                 src_ref=plane.at[part],
                 dst_ref=plane.at[part],
                 send_sem=send_sems.at[2],
                 recv_sem=recv_sems.at[2],
-                device_id=to,
+                device_id={"ctx": ctx, "tp": tp},
                 device_id_type=MESH,
             ).start()
 
-        @pl.loop(2, 2 * chips)
+        @pl.loop(1, n_tp)
         def _(off):
-            tell(in_plane(lax.rem(2 * spot + off, 2 * chips), 2, 0))
-
-        tell(in_plane(2 * spot + 1, 2, 0))
+            tp = lax.rem(mt + off, n_tp)
+            for half_at in (over, here):
+                for core in range(2):
+                    tell(half_at + core, tp)
+
+        tell(over, mt)
+        tell(over + 1, mt)
+        tell(here + 1, mt)
 
         @pl.when(jnp.logical_not(ground))
         def _():
-            tell(in_plane(2 * spot, 2, 0))
-
-        @pl.loop(0, CTX)
+            tell(here, mt)
+
+        @pl.loop(0, half_ctx)
         def _(off):
-            to = lax.rem(upper + off, 2) * half_ctx + off // 2
-            for src, dst, which in (
-                (send2.at[group(to, BACK), :], recv2.at[group(slot, BACK), :], 1),
-                (send3, recv3.at[group(slot, ORDER), :], 5),
-            ):
-                pltpu.make_async_remote_copy(
-                    src_ref=src,
-                    dst_ref=dst,
-                    send_sem=send_sems.at[which],
-                    recv_sem=recv_sems.at[which],
-                    device_id={"ctx": to, "tp": there},
-                    device_id_type=MESH,
-                ).start()
+            for half_at in (over, here):
+                to = half_at + off
+                for src, dst, which in (
+                    (send2.at[group(to, BACK), :], recv2.at[group(slot, BACK), :], 1),
+                    (send3, recv3.at[group(slot, ORDER), :], 5),
+                ):
+                    pltpu.make_async_remote_copy(
+                        src_ref=src,
+                        dst_ref=dst,
+                        send_sem=send_sems.at[which],
+                        recv_sem=recv_sems.at[which],
+                        device_id={"ctx": to, "tp": there},
+                        device_id_type=MESH,
+                    ).start()
 
     wait_bytes(recv2, recv_sems.at[1])
 
@@ -375,7 +384,7 @@
                     dst_ref=column,
                     send_sem=send_sems.at[3],
                     recv_sem=recv_sems.at[3],
-                    device_id={"ctx": upper * half_ctx + off},
+                    device_id={"ctx": here + off},
                     device_id_type=MESH,
                 ).start()
 

time: 30.1 us -> 29.3 us (0.973)
  Pallas kernels: 29 us -> 28.1 us
    pallas_call x1, Pallas kernels: 28.1 us -> 27.3 us  [shards(): pl.pallas_call(kernel, out_shape=(line, line, line, line, pltpu.VMEM((ORD...]
where the time goes in v5:
time: 29.3 us; the launch traced here: 28.7 us
  Pallas kernels  28.1 us (96%)
  between operations  0.64 us (2%)
    pallas_call x1, Pallas kernels, shards(): pl.pallas_call(kernel, out_shape=(line, line, line, line, pltpu.VMEM((ORD...  27.3 us
    pallas_call x1, Pallas kernels, shards(): pl.pallas_call(write, out_shape=tuple((jax.ShapeDtypeStruct(o.shape, o.dt...  0.83 us

profile of v5, /device:TPU:1, one launch (start us, length us, event | category | flops | bytes accessed | tf_op | source)
XLA Modules:
  0.0 28.7 jit_solution(12081750452030174485)
XLA Ops:
  0.6 27.3 %modal_conv.1 = (bf16[128,512]{1,0:T(8,128)(2,1)S(1)}, bf16[128,512]{1,0:T(8,128)(2,1)S(1)}, bf16[128,512]{1,0:T(8,128)(2,1)S(1)}, bf16[128,512]{1,0:T(8,128)(2,1)S(1)}, f32[16,512]{1,0:T(8,128)S(1)}) custom-call(bf16[128,512]{1,0:T(8,128)(2,1)} %q_hbm.1, bf16[128,512]{1,0:T(8,128)(2,1)} %k_hbm.1, bf16[128,512]{1,0:T(8,128)(2,1)} %v_hbm.1, ...), custom_call_target="tpu_custom_call" | custom-call | tf_op jit(solution)/shard_map/modal_conv/pallas_call | solution.py:436
  27.9 0.8 %write_out.1 = (bf16[128,512]{1,0:T(8,128)(2,1)}, bf16[128,512]{1,0:T(8,128)(2,1)}, bf16[128,512]{1,0:T(8,128)(2,1)}, bf16[128,512]{1,0:T(8,128)(2,1)}, f32[16,512]{1,0:T(8,128)}) custom-call(bf16[128,512]{1,0:T(8,128)(2,1)S(1)} %get-tuple-element.15.refs_0_, bf16[128,512]{1,0:T(8,128)(2,1)S(1)} %get-tuple-element.16.refs_1_, ...), custom_call_target="tpu_custom_call" | custom-call | tf_op jit(solution)/shard_map/write_out/pallas_call | solution.py:472

commit v6 on v5

--- a/solution.py
+++ b/solution.py
@@ -39,7 +39,6 @@
     owner = (floor < PLANES) & (lax.rem(line, 2) == 0)
     there = lax.rem(mt + n_tp // 2, n_tp)
     slot = upper * PLANES + floor
-    spot = upper * n_tp + mt
     rows, chans = q_in.shape
     cts = chans // LANES
 
@@ -57,7 +56,7 @@
 
     barrier = pltpu.get_barrier_semaphore()
 
-    ground = floor == 0
+    head = line == 1
 
     here, over = upper * half_ctx, (1 - upper) * half_ctx
 
@@ -71,25 +70,14 @@
             signal(over + off, there)
             signal(here + off, there)
 
-    is_target = ground & owner
-
-    @pl.when(ground)
-    def _():
-        @pl.loop(1, n_tp)
+    @pl.when(head)
+    def _():
+        @pl.loop(0, n_tp)
         def _(off):
             tp = lax.rem(mt + off, n_tp)
             for z in range(PLANES):
                 signal(over + 2 * z, tp)
                 signal(here + 2 * z, tp)
-
-        signal(over, mt)
-        for z in range(1, PLANES):
-            signal(over + 2 * z, mt)
-            signal(here + 2 * z, mt)
-
-        @pl.when(jnp.logical_not(owner))
-        def _():
-            signal(here, mt)
 
     def lanes(ct):
         return pl.ds(ct * LANES, LANES)
@@ -154,13 +142,9 @@
     def tile(index):
         return pl.ds(pl.multiple_of(index * ROWS, ROWS), ROWS)
 
-    @pl.when(is_target)
-    def _():
-        pl.semaphore_wait(barrier, OWNERS + 2 * chips - 1)
-
-    @pl.when(owner & jnp.logical_not(ground))
-    def _():
-        pl.semaphore_wait(barrier, OWNERS + 2 * chips)
+    @pl.when(owner)
+    def _():
+        pl.semaphore_wait(barrier, OWNERS + chips)
 
     @pl.when(jnp.logical_not(owner))
     def _():
@@ -267,19 +251,16 @@
             return recv1[pl.ds(e * POST + i * ORDER, ORDER), :].astype(f32)
 
         zero = jnp.zeros((ORDER, LANES), f32)
-        carry, back, cross, inside = zero, zero, zero, zero
+        carry, cross, inside = zero, zero, zero
         for e in range(CTX):
-            last = CTX - 1 - e
             send2[pl.ds(e * BACK, ORDER), :] = carry.astype(bf16)
-            send2[pl.ds(last * BACK + ORDER, ORDER), :] = back.astype(bf16)
             cross = cross + came(e, 1) * carry
             inside = inside + came(e, 2)
             carry = carry * block + came(e, 0)
-            back = back * block + came(last, 1)
         raw = scale * (inside + step * cross)
         send3[...] = raw
 
-        part = floor * chips + spot
+        part = (upper * PLANES + floor) * n_tp + mt
         plane[part] = jnp.sum(raw * raw, axis=0, keepdims=True)
 
         def tell(ctx, tp):
@@ -292,20 +273,16 @@
                 device_id_type=MESH,
             ).start()
 
-        @pl.loop(1, n_tp)
-        def _(off):
-            tp = lax.rem(mt + off, n_tp)
-            for half_at in (over, here):
-                for core in range(2):
-                    tell(half_at + core, tp)
-
-        tell(over, mt)
-        tell(over + 1, mt)
-        tell(here + 1, mt)
-
-        @pl.when(jnp.logical_not(ground))
-        def _():
-            tell(here, mt)
+        for half_at in (0, half_ctx):
+
+            @pl.loop(0, n_tp)
+            def _(tp):
+                tell(half_at + 1, tp)
+
+        carry = zero
+        for e in reversed(range(CTX)):
+            send2[pl.ds(e * BACK + ORDER, ORDER), :] = carry.astype(bf16)
+            carry = carry * block + came(e, 1)
 
         @pl.loop(0, half_ctx)
         def _(off):
@@ -363,32 +340,31 @@
             gk_out[at] = (v_in[at].astype(jnp.float32) * grad).astype(jnp.bfloat16)
             gv_out[at] = (k_in[at].astype(jnp.float32) * grad).astype(jnp.bfloat16)
 
-    @pl.when(ground)
-    def _():
-        @pl.when(owner)
-        def _():
-            wait_bytes(plane.at[pl.ds(0, 2 * chips - 1)], recv_sems.at[2])
-
-        @pl.when(jnp.logical_not(owner))
-        def _():
-            wait_bytes(plane, recv_sems.at[2])
-
-        column[...] = jnp.sum(plane[...], axis=0)
-
-        @pl.when(owner)
-        def _():
-            @pl.loop(2, half_ctx)
-            def _(off):
-                pltpu.make_async_remote_copy(
-                    src_ref=column,
-                    dst_ref=column,
-                    send_sem=send_sems.at[3],
-                    recv_sem=recv_sems.at[3],
-                    device_id={"ctx": here + off},
-                    device_id_type=MESH,
-                ).start()
-
-    @pl.when(jnp.logical_not(ground))
+    @pl.when(head)
+    def _():
+        wait_bytes(plane, recv_sems.at[2])
+        sums = [plane[i] for i in range(n_tp * 2 * PLANES)]
+        while len(sums) > 1:
+            sums = [a + b for a, b in zip(sums[::2], sums[1::2])]
+        column[...] = sums[0]
+
+        def hand(to):
+            pltpu.make_async_remote_copy(
+                src_ref=column,
+                dst_ref=column,
+                send_sem=send_sems.at[3],
+                recv_sem=recv_sems.at[3],
+                device_id={"ctx": to},
+                device_id_type=MESH,
+            ).start()
+
+        @pl.loop(2, half_ctx)
+        def _(off):
+            hand(here + off)
+
+        hand(here)
+
+    @pl.when(jnp.logical_not(head))
     def _():
         wait_bytes(column, recv_sems.at[3])
 
@@ -404,15 +380,11 @@
         rate_copy.wait_send()
         wait_bytes(send2, send_sems.at[1])
         wait_bytes(xs.at[pl.ds(0, CTX * ORDER), :], send_sems.at[5])
-
-    @pl.when(is_target)
-    def _():
-        wait_bytes(plane.at[pl.ds(0, 2 * chips - 1)], send_sems.at[2])
-        wait_bytes(plane.at[pl.ds(0, half_ctx - 2)], send_sems.at[3])
-
-    @pl.when(owner & jnp.logical_not(ground))
-    def _():
-        wait_bytes(plane, send_sems.at[2])
+        wait_bytes(plane.at[pl.ds(0, chips)], send_sems.at[2])
+
+    @pl.when(head)
+    def _():
+        wait_bytes(plane.at[pl.ds(0, half_ctx - 1)], send_sems.at[3])
 
 
 def write(*refs):

time: 29.3 us -> 29.3 us (level); the launches traced: 28.7 us -> 29.1 us
  Pallas kernels: 28.1 us -> 28.4 us
    pallas_call x1, Pallas kernels: 27.3 us -> 27.6 us  [shards(): pl.pallas_call(kernel, out_shape=(line, line, line, line, pltpu.VMEM((ORD...]
where the time goes in v6:
time: 29.3 us; the launch traced here: 29.1 us
  Pallas kernels  28.4 us (97%)
  between operations  0.64 us (2%)
    pallas_call x1, Pallas kernels, shards(): pl.pallas_call(kernel, out_shape=(line, line, line, line, pltpu.VMEM((ORD...  27.6 us
    pallas_call x1, Pallas kernels, shards(): pl.pallas_call(write, out_shape=tuple((jax.ShapeDtypeStruct(o.shape, o.dt...  0.83 us

profile of v6, /device:TPU:1, one launch (start us, length us, event | category | flops | bytes accessed | tf_op | source)
XLA Modules:
  0.0 29.1 jit_solution(6582784559066570996)
XLA Ops:
  0.6 27.6 %modal_conv.1 = (bf16[128,512]{1,0:T(8,128)(2,1)S(1)}, bf16[128,512]{1,0:T(8,128)(2,1)S(1)}, bf16[128,512]{1,0:T(8,128)(2,1)S(1)}, bf16[128,512]{1,0:T(8,128)(2,1)S(1)}, f32[16,512]{1,0:T(8,128)S(1)}) custom-call(bf16[128,512]{1,0:T(8,128)(2,1)} %q_hbm.1, bf16[128,512]{1,0:T(8,128)(2,1)} %k_hbm.1, bf16[128,512]{1,0:T(8,128)(2,1)} %v_hbm.1, ...), custom_call_target="tpu_custom_call" | custom-call | tf_op jit(solution)/shard_map/modal_conv/pallas_call | solution.py:408
  28.2 0.8 %write_out.1 = (bf16[128,512]{1,0:T(8,128)(2,1)}, bf16[128,512]{1,0:T(8,128)(2,1)}, bf16[128,512]{1,0:T(8,128)(2,1)}, bf16[128,512]{1,0:T(8,128)(2,1)}, f32[16,512]{1,0:T(8,128)}) custom-call(bf16[128,512]{1,0:T(8,128)(2,1)S(1)} %get-tuple-element.15.refs_0_, bf16[128,512]{1,0:T(8,128)(2,1)S(1)} %get-tuple-element.16.refs_1_, ...), custom_call_target="tpu_custom_call" | custom-call | tf_op jit(solution)/shard_map/write_out/pallas_call | solution.py:444
